TPU v7x, 256 devices: a whole 4x4x8 slice. The times are simulated.
256 devices in a mesh: tm: 32 (over z, x), trk: 8 (over y, core).
Axes of the slice: x: 4, y: 4, z: 8, core: 2. Of those that a mesh axis runs over, the one named last changes fastest.
Arguments:
- track_embed: bfloat16 [8192, 1024], P(('tm', 'trk')), may hold values from -6 to 6
- view_ids: int32 [8192, 16], P(('tm', 'trk')), may hold values from 0 to 255, all different within a row; in each aligned block of 32 rows (0 to 31, 32 to 63, ...) at most 4 rows name the same one
- view_count: int32 [8192], P(('tm', 'trk')), may hold values from 1 to 16
- key_feats: bfloat16 [32, 8, 512, 1024], P('tm', 'trk'), may hold values from -160 to 160
- value_feats: bfloat16 [32, 8, 512, 1024], P('tm', 'trk'), may hold values from -6 to 6
- track_gain: float32 [1024], replicated, may hold values from 0.5 to 1.5
- w_temporal: bfloat16 [1024, 3072], replicated, may hold values from -0.1875 to 0.1875
- temporal_scale: float32 [8], replicated, may hold values from 0.5 to 40
- w_merge: bfloat16 [1024, 1024], replicated, may hold values from -0.1875 to 0.1875
- box_gain: float32 [1024], replicated, may hold values from 0.5 to 1.5
- w_hidden: bfloat16 [1024, 512], replicated, may hold values from -0.1875 to 0.1875
- b_hidden: float32 [512], replicated, may hold values from -4 to 4
- w_box: bfloat16 [512, 10], replicated, may hold values from -0.25 to 0.25
Outputs:
- refined: bfloat16 [8192, 16, 1024], P(('tm', 'trk'))
- boxes: float32 [8192, 16, 10], P(('tm', 'trk'))
Inputs may be any that keep to these rules, and one draw needn't show every extreme that they name: `view_ids`: entry v stands for frame v // 8 seen by camera v % 8. The 16 entries of one track are distinct. Counting padding entries too, at most 4 of the tracks of one device name any one view, and in some of the devices exactly 4 name one view. Only the first view_count entries of a track's list are visible; the others are padding.
All inputs are finite; a program needn't handle non-finite values.
Results may differ from a plain program's by a relative error of at most 0.0055.
The roundings to bfloat16 on the way count: a program that leaves them out, or rounds other values in their place, can miss the bound.
Values may be sent and summed in bfloat16 or wider, within the bound.
A program may use at most 64 MiB of HBM per device.

v0:
```python
import math

import jax
import jax.numpy as jnp
from jax import lax
from jax.sharding import PartitionSpec as P

HEADS = 8
CAMS = 8


epsilon = 1e-05
masked_score = -1e30


def split_up(x, dim, count):
    lengths = x.shape
    blocks = x.reshape(*lengths[:dim], count, lengths[dim] // count, *lengths[dim + 1 :])
    return jnp.moveaxis(blocks, dim, 0)


def in_order(blocks, dim):
    lengths = list(blocks.shape[1:])
    lengths[dim] *= blocks.shape[0]
    return jnp.moveaxis(blocks, 0, dim).reshape(lengths)


def one_exchange(x, axis, axes, splits, concats):
    sizes = [lax.axis_size(a) for a in axes]
    blocks = split_up(x, splits[0], sizes[0])
    blocks = jnp.moveaxis(split_up(blocks, splits[1] + 1, sizes[1]), 0, 1)
    inside = blocks.shape[2:]
    blocks = blocks.reshape(-1, *inside)
    blocks = lax.all_to_all(blocks, axis, split_axis=0, concat_axis=0, tiled=True)
    blocks = in_order(blocks.reshape(*sizes, *inside), concats[0] + 1)
    return in_order(blocks, concats[1])


def from_behind(block, axis, distance):
    devices = range(lax.axis_size(axis))
    route = [((i - distance) % len(devices), i) for i in devices]
    return lax.ppermute(block, axis, route)


def layer_norm(values):
    centre = jnp.mean(values, axis=-1, keepdims=True)
    shifted = values - centre
    spread = jnp.mean(shifted * shifted, axis=-1, keepdims=True)
    return shifted * lax.rsqrt(spread + epsilon)


def time_code(frame_ids, model_width):
    half_width = model_width // 2
    freq_index = jnp.arange(half_width).astype(jnp.float32)
    freq_rates = jnp.exp(freq_index * (-2.0 * math.log(10000.0) / model_width))
    angles = frame_ids.astype(jnp.float32)[..., None] * freq_rates
    return jnp.concatenate([jnp.sin(angles), jnp.cos(angles)], axis=-1)


def attend_views(arrived, view_keys, view_values):
    model_width = arrived.shape[-1]
    head_feature_width = model_width // HEADS
    score_scale = head_feature_width ** (-0.5)

    def one_head(head_index):
        head_start = head_index * head_feature_width
        query_part = lax.dynamic_slice_in_dim(arrived, head_start, head_feature_width, 3)
        key_part = lax.dynamic_slice_in_dim(view_keys, head_start, head_feature_width, 2)
        value_part = lax.dynamic_slice_in_dim(view_values, head_start, head_feature_width, 2)
        attention_scores = (
            jnp.einsum("slcd,lpd->lscp", query_part, key_part, preferred_element_type=jnp.float32)
            * score_scale
        )
        row_top = jnp.max(attention_scores, axis=-1, keepdims=True)
        weights = jnp.exp(attention_scores - row_top)
        totals = jnp.sum(weights, axis=-1, keepdims=True)
        softmax_numerator = jnp.einsum(
            "lscp,lpd->lscd",
            weights.astype(jnp.bfloat16),
            value_part,
            preferred_element_type=jnp.float32,
        )
        return (softmax_numerator / totals).astype(jnp.bfloat16)

    per_head = lax.map(one_head, jnp.arange(HEADS, dtype=jnp.int32))
    merged = jnp.transpose(per_head, (2, 1, 3, 0, 4))
    return merged.reshape(arrived.shape)


def track_block(
    states,
    attended,
    counts,
    w_temporal,
    temporal_scale,
    w_merge,
    box_gain,
    w_hidden,
    b_hidden,
    w_box,
):
    track_rows = states.shape[0]
    list_length = attended.shape[1]
    model_width = states.shape[1]
    head_feature_width = model_width // HEADS
    residual_rows = states[:, None, :] + attended.astype(jnp.float32)
    normed = layer_norm(residual_rows).astype(jnp.bfloat16)
    projected = jnp.dot(
        normed.reshape(track_rows * list_length, model_width),
        w_temporal,
        preferred_element_type=jnp.float32,
    ).astype(jnp.bfloat16)
    projected = projected.reshape(track_rows, list_length, 3, HEADS, head_feature_width)
    per_head_queries = projected[:, :, 0]
    per_head_keys = projected[:, :, 1]
    per_head_values = projected[:, :, 2]
    attention_scores = jnp.einsum(
        "bqhd,bkhd->bhqk", per_head_queries, per_head_keys, preferred_element_type=jnp.float32
    )
    attention_scores = attention_scores * (
        temporal_scale[None, :, None, None] * head_feature_width ** (-0.5)
    )
    positions = jnp.arange(list_length)
    key_valid = positions[None, :] < counts[:, None]
    attention_scores = jnp.where(key_valid[:, None, None, :], attention_scores, masked_score)
    row_top = jnp.max(attention_scores, axis=-1, keepdims=True)
    weights = jnp.exp(attention_scores - row_top)
    probs = (weights / jnp.sum(weights, axis=-1, keepdims=True)).astype(jnp.bfloat16)
    mixed_heads = jnp.einsum(
        "bhqk,bkhd->bqhd", probs, per_head_values, preferred_element_type=jnp.float32
    ).astype(jnp.bfloat16)
    mixed_heads = mixed_heads.reshape(track_rows * list_length, model_width)
    updated = residual_rows + jnp.dot(
        mixed_heads, w_merge, preferred_element_type=jnp.float32
    ).reshape(track_rows, list_length, model_width)
    row_valid = key_valid.astype(jnp.float32)[:, :, None]
    refined = (updated * row_valid).astype(jnp.bfloat16)
    box_input = (layer_norm(updated) * box_gain).astype(jnp.bfloat16)
    box_hidden = jax.nn.gelu(
        jnp.dot(
            box_input.reshape(track_rows * list_length, model_width),
            w_hidden,
            preferred_element_type=jnp.float32,
        )
        + b_hidden
    ).astype(jnp.bfloat16)
    box_values = (
        jnp.dot(box_hidden, w_box, preferred_element_type=jnp.float32).reshape(
            track_rows, list_length, w_box.shape[1]
        )
        * row_valid
    )
    return (refined, box_values)


def local(
    track_embed,
    view_ids,
    view_count,
    key_feats,
    value_feats,
    track_gain,
    w_temporal,
    temporal_scale,
    w_merge,
    box_gain,
    w_hidden,
    b_hidden,
    w_box,
):
    tm_count = lax.axis_size("tm")
    trk_count = lax.axis_size("trk")
    local_frames = key_feats.shape[0]
    local_cameras = key_feats.shape[1]
    pixel_count = key_feats.shape[2]
    model_width = track_embed.shape[1]
    track_local = track_embed.shape[0]
    list_length = view_ids.shape[1]
    row_local = track_local * list_length
    view_total = local_frames * tm_count * CAMS
    capacity = max(2, (2 * row_local + view_total - 1) // view_total)
    local_views = local_frames * local_cameras
    states = layer_norm(track_embed.astype(jnp.float32)) * track_gain
    frame_ids = view_ids // CAMS
    queries = (states[:, None, :] + time_code(frame_ids, model_width)).astype(jnp.bfloat16)
    queries = queries.reshape(row_local, model_width)
    flat_views = view_ids.reshape(row_local)
    camera_ids = flat_views % CAMS
    flat_frames = flat_views // CAMS
    target_tm = flat_frames // local_frames
    target_trk = camera_ids // local_cameras
    local_view = flat_frames % local_frames * local_cameras + camera_ids % local_cameras
    position = jnp.arange(row_local, dtype=jnp.int32)
    earlier = (flat_views[:, None] == flat_views[None, :]) & (position[None, :] < position[:, None])
    slot_rank = jnp.sum(earlier.astype(jnp.int32), axis=1)
    slot_index = (
        (target_tm * trk_count + target_trk) * local_views + local_view
    ) * capacity + slot_rank
    slot_total = tm_count * trk_count * local_views * capacity
    outbound = jnp.zeros((slot_total, model_width), jnp.bfloat16).at[slot_index].set(queries)
    outbound = outbound.reshape(tm_count, trk_count, local_views * capacity, model_width)
    received = one_exchange(outbound, ("tm", "trk"), ("tm", "trk"), (0, 1), (0, 1))
    next_key, next_value = from_behind((key_feats, value_feats), "trk", -1)
    next_keys = jnp.concatenate([key_feats[:, 1:], next_key], axis=1)
    next_values = jnp.concatenate([value_feats[:, 1:], next_value], axis=1)
    view_keys = jnp.concatenate([key_feats, next_keys], axis=2).reshape(
        local_views, 2 * pixel_count, model_width
    )
    view_values = jnp.concatenate([value_feats, next_values], axis=2).reshape(
        local_views, 2 * pixel_count, model_width
    )
    arrived = received.reshape(tm_count * trk_count, local_views, capacity, model_width)
    answered = attend_views(arrived, view_keys, view_values)
    answered = answered.reshape(tm_count, trk_count, local_views * capacity, model_width)
    returned = one_exchange(answered, ("tm", "trk"), ("tm", "trk"), (0, 1), (0, 1))
    attended = returned.reshape(slot_total, model_width)[slot_index].reshape(
        track_local, list_length, model_width
    )
    refined, box_values = track_block(
        states,
        attended,
        view_count,
        w_temporal,
        temporal_scale,
        w_merge,
        box_gain,
        w_hidden,
        b_hidden,
        w_box,
    )
    return (refined, box_values)


def solution(mesh):
    placed = (
        P(("tm", "trk"), None),
        P(("tm", "trk"), None),
        P(("tm", "trk")),
        P("tm", "trk", None, None),
        P("tm", "trk", None, None),
        P(),
        P(),
        P(),
        P(),
        P(),
        P(),
        P(),
        P(),
    )
    return jax.shard_map(
        local,
        mesh=mesh,
        in_specs=placed,
        out_specs=(P(("tm", "trk"), None, None), P(("tm", "trk"), None, None)),
        check_vma=False,
    )
```

profile of v0, /device:TPU:33, one launch (start us, length us, event | category | flops | bytes accessed | tf_op | source)
XLA Modules:
  0.0 249.7 jit_solution(3223927057604573253)
XLA Ops:
  5.8 3.7 %multiply_sine_fusion = (f32[512,512]{1,0:T(8,128)S(1)}, f32[512,512]{1,0:T(8,128)S(1)}) fusion(f32[512]{0:T(512)S(1)} %multiply_exponential_fusion, f32[512]{0:T(512)S(1)} %mul.172), kind=kLoop, calls=%fused_computation.50 | loop fusion | flops 262144 | bytes 2101248 | tf_op jit(solution)/shard_map/sin | solution.py:57
  9.9 4.2 %scatter_custom_fusion = bf16[1024,1024]{1,0:T(8,128)(2,1)} fusion(s32[512]{0:T(512)S(1)} %bitcast.123, bf16[512,1024]{1,0:T(8,128)(2,1)S(1)} %fusion.26, bf16[]{:T(256)} %constant.111.clone.1), kind=kCustom, calls=%fused_computation.74 | custom fusion | bytes 2097154 | tf_op jit(solution)/shard_map/scatter | solution.py:200
  14.0 4.1 %reshape_transpose_transpose_reshape_reshape_reshape.3 = bf16[256,1,1,4,1024]{4,3,0,2,1:T(4,128)(2,1)} reshape(bf16[1024,1024]{1,0:T(8,128)(2,1)} %scatter_custom_fusion) | data formatting | bytes 4194304 | tf_op jit(solution)/shard_map/reshape;transpose;transpose;reshape;reshape;reshape | solution.py:33
  18.1 15.7 %all-to-all-start = ((bf16[256,1,1,4,1024]{4,3,2,1,0:T(4,128)(2,1)}), bf16[256,1,1,4,1024]{4,3,2,1,0:T(4,128)(2,1)}, u32[]{:S(2)}, u32[]{:S(2)}) async-start(bf16[256,1,1,4,1024]{4,3,2,1,0:T(4,128)(2,1)} %bitcast.118), calls=%async_computation | async-start | bytes 4194304 | tf_op jit(solution)/shard_map/all_to_all | solution.py:34
  34.2 2.6 %collective-permute-start.1 = (bf16[1,1,512,1024]{3,2,1,0:T(8,128)(2,1)}, bf16[1,1,512,1024]{3,2,1,0:T(8,128)(2,1)}, u32[]{:S(2)}, u32[]{:S(2)}) collective-permute-start(bf16[1,1,512,1024]{3,2,1,0:T(8,128)(2,1)} %param.19), channel_id=1, source_target_pairs={{1,0},{2,1},{3,2},{4,3},{5,4},{6,5},{7,6},{0,7},{9,8},{10,9},{11,1... | collective-permute-start | bytes 3145736 | tf_op jit(solution)/shard_map/ppermute | solution.py:42
  36.9 22.0 %collective-permute-done = bf16[1,1,512,1024]{3,2,1,0:T(8,128)(2,1)} collective-permute-done((bf16[1,1,512,1024]{3,2,1,0:T(8,128)(2,1)S(1)}, bf16[1,1,512,1024]{3,2,1,0:T(8,128)(2,1)}, u32[]{:S(2)}, u32[]{:S(2)}) %collective-permute-start) | collective-permute-done | bytes 1048608 | tf_op jit(solution)/shard_map/ppermute | solution.py:42
  58.9 2.7 %maximum_bitcast_fusion = bf16[1,1024,1024]{2,1,0:T(8,128)(2,1)} fusion(bf16[1,1,512,1024]{3,2,1,0:T(8,128)(2,1)} %collective-permute-done, bf16[1,1,512,1024]{3,2,1,0:T(8,128)(2,1)S(1)} %copy-done.2), kind=kLoop, calls=%fused_computation.31 | loop fusion | flops 4194304 | bytes 4194304 | tf_op jit(solution)/shard_map/reshape | solution.py:206
  61.6 17.3 %collective-permute-done.1 = bf16[1,1,512,1024]{3,2,1,0:T(8,128)(2,1)} collective-permute-done((bf16[1,1,512,1024]{3,2,1,0:T(8,128)(2,1)}, bf16[1,1,512,1024]{3,2,1,0:T(8,128)(2,1)}, u32[]{:S(2)}, u32[]{:S(2)}) %collective-permute-start.1) | collective-permute-done | bytes 1048608 | tf_op jit(solution)/shard_map/ppermute | solution.py:42
  78.9 2.7 %maximum_bitcast_fusion.1 = bf16[1,1024,1024]{2,1,0:T(8,128)(2,1)} fusion(bf16[1,1,512,1024]{3,2,1,0:T(8,128)(2,1)} %collective-permute-done.1, bf16[1,1,512,1024]{3,2,1,0:T(8,128)(2,1)S(1)} %copy-done.3), kind=kLoop, calls=%fused_computation.32 | loop fusion | flops 4194304 | bytes 4194304 | tf_op jit(solution)/shard_map/reshape | solution.py:209
  81.6 3.4 %all-to-all-done = bf16[256,1,1,4,1024]{4,3,2,1,0:T(4,128)(2,1)} async-done(((bf16[256,1,1,4,1024]{4,3,2,1,0:T(4,128)(2,1)}), bf16[256,1,1,4,1024]{4,3,2,1,0:T(4,128)(2,1)}, u32[]{:S(2)}, u32[]{:S(2)}) %all-to-all-start) | async-done | bytes 2097184 | tf_op jit(solution)/shard_map/all_to_all | solution.py:34
  85.0 3.6 %copy.107 = bf16[32,8,1,4,1024]{4,1,0,3,2:T(8,128)(2,1)} copy(bf16[32,8,1,4,1024]{4,3,1,0,2:T(4,128)(2,1)} %bitcast.14) | data formatting | bytes 4194304 | tf_op jit(solution)/shard_map/transpose | solution.py:25
  88.5 53.7 %while.10 = (s32[]{:T(128)}, bf16[8,1,256,4,128]{2,4,0,3,1:T(8,128)(2,1)}, s32[8]{0:T(128)S(1)}, bf16[256,1,4,1024]{3,0,2,1:T(8,128)(2,1)}, bf16[1,1024,1024]{2,...) while((s32[]{:T(128)}, ...), condition=%wide.region_7.8_spmd, body=%wide.region_4.7_spmd.sunk | while | flops 545519616 | bytes 14702243 | solution.py:85
  89.8 1.8 multiply_reduce_fusion.4
  96.5 1.8 multiply_reduce_fusion.4
  103.2 1.8 multiply_reduce_fusion.4
  109.9 1.8 multiply_reduce_fusion.4
  116.6 1.8 multiply_reduce_fusion.4
  130.0 1.8 multiply_reduce_fusion.4
  136.7 1.8 multiply_reduce_fusion.4
  142.2 4.6 %copy.67 = bf16[256,1,1,4,1024]{4,3,2,1,0:T(4,128)(2,1)} copy(bf16[256,1,1,4,1024]{0,4,3,2,1:T(8,128)(2,1)} %bitcast.121) | data formatting | bytes 4194304 | tf_op jit(solution)/shard_map/reshape;transpose;transpose;reshape;reshape;reshape;reshape | solution.py:33
  146.7 10.7 %all-to-all-start.1 = ((bf16[256,1,1,4,1024]{4,3,2,1,0:T(4,128)(2,1)}), bf16[256,1,1,4,1024]{4,3,2,1,0:T(4,128)(2,1)}, u32[]{:S(2)}, u32[]{:S(2)}) async-start(bf16[256,1,1,4,1024]{4,3,2,1,0:T(4,128)(2,1)} %copy.67), calls=%async_computation.1 | async-start | bytes 4194304 | tf_op jit(solution)/shard_map/all_to_all | solution.py:34
  157.5 51.0 %all-to-all-done.1 = bf16[256,1,1,4,1024]{4,3,2,1,0:T(4,128)(2,1)} async-done(((bf16[256,1,1,4,1024]{4,3,2,1,0:T(4,128)(2,1)}), bf16[256,1,1,4,1024]{4,3,2,1,0:T(4,128)(2,1)}, u32[]{:S(2)}, u32[]{:S(2)}) %all-to-all-start.1) | async-done | bytes 2097184 | tf_op jit(solution)/shard_map/all_to_all | solution.py:34
  208.5 2.2 copy.106
  210.7 3.3 %copy.69 = bf16[32,8,1,4,1024]{4,3,1,0,2:T(4,128)(2,1)} copy(bf16[32,8,1,4,1024]{4,1,0,3,2:T(8,128)(2,1)S(1)} %bitcast.119) | data formatting | bytes 4194304 | tf_op jit(solution)/shard_map/transpose | solution.py:25
  214.0 4.0 %reshape_reshape.7 = bf16[1024,1024]{1,0:T(8,128)(2,1)} reshape(bf16[32,8,1,4,1024]{4,3,1,0,2:T(4,128)(2,1)} %copy.69) | data formatting | bytes 4194304 | tf_op jit(solution)/shard_map/reshape;reshape | solution.py:216
  218.0 4.6 %gather_fusion = bf16[512,1024]{1,0:T(8,128)(2,1)S(1)} fusion(bf16[1024,1024]{1,0:T(8,128)(2,1)} %reshape_reshape.7, s32[1024]{0:T(1024)S(1)} %pad_clamp_fusion), kind=kCustom, calls=%fused_computation | custom fusion | bytes 2099200 | tf_op jit(solution)/shard_map/gather | solution.py:216
  224.2 2.0 multiply_reduce_fusion.2
  226.7 6.7 %fusion.32 = bf16[64,8,24,128]{3,1,2,0:T(8,128)(2,1)S(1)} fusion(bf16[512,1024]{1,0:T(8,128)(2,1)S(1)} %fusion.29, bf16[1024,3072]{1,0:T(8,128)(2,1)} %param.21), kind=kOutput, calls=%fused_computation.44 | convolution fusion | flops 3222798336 | bytes 10485760 | tf_op jit(solution)/shard_map/dot_general | solution.py:108
  234.3 2.3 fusion.75
  236.6 4.1 %fusion.76 = (f32[32,8,16]{2,1,0:T(8,128)S(1)}, f32[32,8,16,16]{2,3,1,0:T(8,128)}) fusion(f32[8]{0:T(128)S(1)} %broadcast_multiply_fusion.3, pred[32,16]{1,0:T(8,128)(4,1)S(1)} %get-tuple-element.67, bf16[32,16,1,8,128]{4,3,2,1,0:T(8,128)(2,1)} %get-tuple-element.61, bf16[32,16,1,8,128]{4,3,2,1,0:T(8,128)(2,1)} %get-tuple-element.60), kind=kOutput, calls=%fused_computation.122 | convolution fusion | flops 17039376 | bytes 2376224 | tf_op jit(solution)/shard_map/sub | solution.py:127
  240.7 2.3 fusion.36
  246.5 2.3 fusion.45
  (95 shorter events, 48.8 us)
Async XLA Ops:
  0.6 242.3 %copy-start = (bf16[1024,1024]{1,0:T(8,128)(2,1)S(1)}, bf16[1024,1024]{1,0:T(8,128)(2,1)}, u32[]{:S(2)}) copy-start(bf16[1024,1024]{1,0:T(8,128)(2,1)} %param.23) | copy-start | bytes 6291460
  18.1 15.7 %copy-start.2 = (bf16[1,1,512,1024]{3,2,1,0:T(8,128)(2,1)S(1)}, bf16[1,1,512,1024]{3,2,1,0:T(8,128)(2,1)}, u32[]{:S(2)}) copy-start(bf16[1,1,512,1024]{3,2,1,0:T(8,128)(2,1)} %param.18) | copy-start | bytes 3145732
  18.1 66.8 %all-to-all-start = ((bf16[256,1,1,4,1024]{4,3,2,1,0:T(4,128)(2,1)}), bf16[256,1,1,4,1024]{4,3,2,1,0:T(4,128)(2,1)}, u32[]{:S(2)}, u32[]{:S(2)}) async-start(bf16[256,1,1,4,1024]{4,3,2,1,0:T(4,128)(2,1)} %bitcast.118), calls=%async_computation | async-start | bytes 4194304 | tf_op jit(solution)/shard_map/all_to_all | solution.py:34
  33.9 25.0 %collective-permute-start = (bf16[1,1,512,1024]{3,2,1,0:T(8,128)(2,1)S(1)}, bf16[1,1,512,1024]{3,2,1,0:T(8,128)(2,1)}, u32[]{:S(2)}, u32[]{:S(2)}) collective-permute-start(bf16[1,1,512,1024]{3,2,1,0:T(8,128)(2,1)S(1)} %copy-done.2), channel_id=1, source_target_pairs={{1,0},{2,1},{3,2},{4,3},{5,4},{6,5},{7,6},{0,7},{9,8},{10,9},{11,1... | collective-permute-start | bytes 3145736 | tf_op jit(solution)/shard_map/ppermute | solution.py:42
  34.2 44.6 %collective-permute-start.1 = (bf16[1,1,512,1024]{3,2,1,0:T(8,128)(2,1)}, bf16[1,1,512,1024]{3,2,1,0:T(8,128)(2,1)}, u32[]{:S(2)}, u32[]{:S(2)}) collective-permute-start(bf16[1,1,512,1024]{3,2,1,0:T(8,128)(2,1)} %param.19), channel_id=1, source_target_pairs={{1,0},{2,1},{3,2},{4,3},{5,4},{6,5},{7,6},{0,7},{9,8},{10,9},{11,1... | collective-permute-start | bytes 3145736 | tf_op jit(solution)/shard_map/ppermute | solution.py:42
  36.9 42.0 %copy-start.3 = (bf16[1,1,512,1024]{3,2,1,0:T(8,128)(2,1)S(1)}, bf16[1,1,512,1024]{3,2,1,0:T(8,128)(2,1)}, u32[]{:S(2)}) copy-start(bf16[1,1,512,1024]{3,2,1,0:T(8,128)(2,1)} %param.19) | copy-start | bytes 3145732
  146.7 10.7 %copy-start.8 = (f32[8]{0:T(128)S(1)}, f32[8]{0:T(128)}, u32[]{:S(2)}) copy-start(f32[8]{0:T(128)} %param.22) | copy-start | bytes 100
  146.7 10.7 %copy-start.5 = (s32[32]{0:T(128)S(1)}, s32[32]{0:T(128)}, u32[]{:S(2)}) copy-start(s32[32]{0:T(128)} %param.17) | copy-start | bytes 388
  146.7 61.8 %all-to-all-start.1 = ((bf16[256,1,1,4,1024]{4,3,2,1,0:T(4,128)(2,1)}), bf16[256,1,1,4,1024]{4,3,2,1,0:T(4,128)(2,1)}, u32[]{:S(2)}, u32[]{:S(2)}) async-start(bf16[256,1,1,4,1024]{4,3,2,1,0:T(4,128)(2,1)} %copy.67), calls=%async_computation.1 | async-start | bytes 4194304 | tf_op jit(solution)/shard_map/all_to_all | solution.py:34
  240.7 2.3 copy-start.1
  244.4 0.7 copy-start.4
  245.1 1.4 copy-start.6
  245.1 1.4 copy-start.7
where the time goes:
time: 253 us; the launch traced here: 250 us
  waiting for transfers between devices  93.6 us (37%)
  local copies, waits for them, and re-layouts  47.7 us (19%)
  matrix products  46 us (18%)
  starting transfers between devices  29.4 us (12%)
  other arithmetic  26.8 us (11%)
  loops' own time  5.36 us (2%)
    all_to_all x2, waiting for transfers between devices, one_exchange(): lax.all_to_all(blocks, axis, split_axis=0, concat_axis=0, tiled=True)  54.4 us
    ppermute x2, waiting for transfers between devices, from_behind(): return lax.ppermute(block, axis, route)  39.2 us
    all_to_all x2, starting transfers between devices, one_exchange(): lax.all_to_all(blocks, axis, split_axis=0, concat_axis=0, tiled=True)  26.4 us
    dot_general x8, matrix products, one_head(): jnp.einsum('slcd,lpd->lscp', query_part, key_part, preferred_element_type...  14.6 us
    dot_general x8, matrix products, one_head(): jnp.einsum('lscp,lpd->lscd', weights.astype(jnp.bfloat16), value_part, pr...  14.6 us
    another operation x2, local copies, waits for them, and re-layouts, one_exchange(): blocks = blocks.reshape(-1, *inside)  8.67 us
    reduce_sum x8, other arithmetic, one_head(): totals = jnp.sum(weights, axis=-1, keepdims=True)  7.44 us
    dynamic_update_slice x16, local copies, waits for them, and re-layouts, attend_views(): per_head = lax.map(one_head, jnp.arange(HEADS, dtype=jnp.int32))  6.97 us
  transfers between devices with their start and end apart: 4, of which 4 were waited for; matrix products, arithmetic and copies ran while one was open for 2% of the time, Pallas kernels for 0%

commit v1 on v0

v1 whole, which is shorter than its diff:
```python
import functools
import math

import jax
import jax.numpy as jnp
from jax import lax
from jax.experimental import pallas as pl
from jax.experimental.pallas import tpu as pltpu
from jax.sharding import PartitionSpec as P

HEADS = 8
CAMS = 8
CAP = 4
NX = 4
EPS = 1e-05
MASKED = -1e30
MESH = pl.DeviceIdType.MESH
BF = jnp.bfloat16
F32 = jnp.float32


def layer_norm(values):
    centre = jnp.mean(values, axis=-1, keepdims=True)
    shifted = values - centre
    spread = jnp.mean(shifted * shifted, axis=-1, keepdims=True)
    return shifted * lax.rsqrt(spread + EPS)


def time_code(frame_ids, model_width):
    half_width = model_width // 2
    freq_index = jnp.arange(half_width).astype(F32)
    freq_rates = jnp.exp(freq_index * (-2.0 * math.log(10000.0) / model_width))
    angles = frame_ids.astype(F32)[..., None] * freq_rates
    return jnp.concatenate([jnp.sin(angles), jnp.cos(angles)], axis=-1)


def iota(shape, dim):
    return lax.broadcasted_iota(jnp.int32, shape, dim)


def nt_dot(a, b):
    return lax.dot_general(a, b, (((1,), (1,)), ((), ())), preferred_element_type=F32)


def tn_dot(a, b):
    return lax.dot_general(a, b, (((0,), (0,)), ((), ())), preferred_element_type=F32)


def place(nt):
    tm = lax.axis_index("tm")
    trk = lax.axis_index("trk")
    z = tm // NX
    x = tm % NX
    return z, x, trk, x * nt + trk


def greet(nz, nt):
    z, x, trk, me = place(nt)
    npl = NX * nt
    barrier = pltpu.get_barrier_semaphore()

    @pl.loop(1, npl)
    def _(k):
        p = lax.rem(me + k, npl)
        pl.semaphore_signal(barrier, inc=1, device_id=(z * NX + p // nt, p % nt), device_id_type=MESH)

    @pl.loop(1, nz)
    def _(k):
        zz = lax.rem(z + k, nz)
        pl.semaphore_signal(barrier, inc=1, device_id=(zz * NX + x, trk), device_id_type=MESH)

    pl.semaphore_wait(barrier, npl - 1 + nz - 1)


def await_bytes(like, sem):
    pltpu.make_async_copy(like, like, sem).wait()


def forward_kernel(
    nz, nt, rows, cap_z,
    embed_ref, ids_ref, code_ref, gain_ref, key_ref, value_ref,
    q_ref, kn_ref, vn_ref, target_ref,
    emb_z, ids_z, q_send,
    z_send, z_recv, zi_send, zi_recv, kv_send, kv_recv, q_ssem, q_rsem, own_sem,
):
    z, x, trk, me = place(nt)
    npl = NX * nt
    width = embed_ref.shape[1]
    cols = nz * rows
    per = nz * CAP
    greet(nz, nt)

    before = (z * NX + x, lax.rem(trk + nt - 1, nt))
    k_copy = pltpu.make_async_remote_copy(
        src_ref=key_ref, dst_ref=kn_ref, send_sem=kv_send.at[0], recv_sem=kv_recv.at[0],
        device_id=before, device_id_type=MESH)
    v_copy = pltpu.make_async_remote_copy(
        src_ref=value_ref, dst_ref=vn_ref, send_sem=kv_send.at[1], recv_sem=kv_recv.at[1],
        device_id=before, device_id_type=MESH)

    own_e = pltpu.make_async_copy(embed_ref, emb_z.at[z], z_recv)
    own_i = pltpu.make_async_copy(ids_ref, ids_z.at[z], zi_recv)
    own_e.start()
    own_i.start()

    @pl.loop(1, nz)
    def _(k):
        zz = lax.rem(z + k, nz)
        to = (zz * NX + x, trk)
        pltpu.make_async_remote_copy(
            src_ref=ids_ref, dst_ref=ids_z.at[z], send_sem=zi_send, recv_sem=zi_recv,
            device_id=to, device_id_type=MESH).start()
        pltpu.make_async_remote_copy(
            src_ref=embed_ref, dst_ref=emb_z.at[z], send_sem=z_send, recv_sem=z_recv,
            device_id=to, device_id_type=MESH).start()

    k_copy.start()
    v_copy.start()

    await_bytes(ids_z, zi_recv)
    ids = ids_z[0]
    for s in range(1, nz):
        ids = jnp.maximum(ids, ids_z[s])
    listing = ids.shape[0]
    view = z * npl + iota((npl, cols), 0)
    named = jnp.zeros((npl, cols), F32)
    for j in range(listing):
        named = jnp.where(ids[j : j + 1, :] == view, 1.0, named)
    named_b = named.astype(BF)
    c0 = iota((cols, cols), 0)
    c1 = iota((cols, cols), 1)
    earlier = jnp.where((c0 < c1) & (c0 // rows == c1 // rows), 1.0, 0.0).astype(BF)
    rank = jnp.dot(named_b, earlier, preferred_element_type=F32)
    ranked = jnp.where(named > 0.5, rank, -1.0)

    zr = iota((per, cols), 0)
    zc = iota((per, cols), 1) // rows
    same_z = zr // CAP == zc
    slot_r = (zr % CAP).astype(F32)
    counts = nt_dot(jnp.where(same_z, 1.0, 0.0).astype(BF), named_b)
    v0 = iota((npl, npl), 0)
    v1 = iota((npl, npl), 1)
    base = jnp.dot(counts.astype(BF), jnp.where(v0 < v1, 1.0, 0.0).astype(BF), preferred_element_type=F32)
    t0 = iota((per, npl), 0)
    tr = (t0 % CAP).astype(F32)
    target_ref[...] = jnp.where(tr < counts, base + tr + ((t0 // CAP) * cap_z).astype(F32), -1.0)

    await_bytes(emb_z, z_recv)
    states = layer_norm(emb_z[...].reshape(cols, width).astype(F32)) * gain_ref[...]
    high = states.astype(BF)
    rest = states - high.astype(F32)
    middle = rest.astype(BF)
    low = (rest - middle.astype(F32)).astype(BF)

    group = 4
    for g in range(npl // group):
        picks = []
        for v in range(g * group, (g + 1) * group):
            picks.append(jnp.where(same_z & (ranked[v : v + 1, :] == slot_r), 1.0, 0.0).astype(BF))
        pick = jnp.concatenate(picks, axis=0)
        made = jnp.dot(pick, high, preferred_element_type=F32)
        made = made + jnp.dot(pick, middle, preferred_element_type=F32)
        made = made + jnp.dot(pick, low, preferred_element_type=F32)
        frame = (g * group) // nt
        made = (made + code_ref[frame : frame + 1, :]).astype(BF)
        q_send[g * group * per : (g + 1) * group * per, :] = made

    mine = pl.ds(pl.multiple_of(me * per, per), per)
    pltpu.make_async_copy(q_send.at[mine], q_ref.at[mine], q_rsem).start()

    @pl.loop(1, npl)
    def _(k):
        p = lax.rem(me + k, npl)
        pltpu.make_async_remote_copy(
            src_ref=q_send.at[pl.ds(pl.multiple_of(p * per, per), per)], dst_ref=q_ref.at[mine],
            send_sem=q_ssem, recv_sem=q_rsem,
            device_id=(z * NX + p // nt, p % nt), device_id_type=MESH).start()

    await_bytes(emb_z.at[pl.ds(0, nz - 1)], z_send)
    await_bytes(ids_z.at[pl.ds(0, nz - 1)], zi_send)
    await_bytes(q_send.at[pl.ds(0, (npl - 1) * per)], q_ssem)
    await_bytes(q_send, q_rsem)
    k_copy.wait()
    v_copy.wait()


def return_kernel(
    nz, nt, cap_z, pair,
    q_ref, k_ref, kn_ref, v_ref, vn_ref, target_ref,
    out_ref,
    a_send, a_recv, moves, b_send,
    a_ssem, a_rsem, b_ssem, b_rsem,
):
    z, x, trk, me = place(nt)
    npl = NX * nt
    per = nz * CAP
    total = npl * per
    tokens = k_ref.shape[0]
    head = 128
    chunks = HEADS // pair
    wide = pair * head
    scale = head ** (-0.5)
    mine = pl.ds(pl.multiple_of(me * per, per), per)
    block = 256
    greet(nz, nt)

    def attend(c):
        @pl.loop(0, total // block)
        def _(b):
            at = pl.ds(pl.multiple_of(b * block, block), block)
            for h in range(pair):
                lanes = slice((c * pair + h) * head, (c * pair + h + 1) * head)
                q = q_ref[at, lanes]
                s0 = nt_dot(q, k_ref[:, lanes])
                s1 = nt_dot(q, kn_ref[:, lanes])
                top = jnp.maximum(jnp.max(s0, axis=-1, keepdims=True), jnp.max(s1, axis=-1, keepdims=True))
                w0 = jnp.exp((s0 - top) * scale)
                w1 = jnp.exp((s1 - top) * scale)
                sums = jnp.sum(w0, axis=-1, keepdims=True) + jnp.sum(w1, axis=-1, keepdims=True)
                o = jnp.dot(w0.astype(BF), v_ref[:, lanes], preferred_element_type=F32)
                o = o + jnp.dot(w1.astype(BF), vn_ref[:, lanes], preferred_element_type=F32)
                a_send[c, at, h * head : (h + 1) * head] = (o / sums).astype(BF)

    def send_in_plane(c):
        pltpu.make_async_copy(a_send.at[c, mine], a_recv.at[c, mine], a_rsem.at[c]).start()

        @pl.loop(1, npl)
        def _(k):
            p = lax.rem(me + k, npl)
            pltpu.make_async_remote_copy(
                src_ref=a_send.at[c, pl.ds(pl.multiple_of(p * per, per), per)], dst_ref=a_recv.at[c, mine],
                send_sem=a_ssem.at[c], recv_sem=a_rsem.at[c],
                device_id=(z * NX + p // nt, p % nt), device_id_type=MESH).start()

    line = pl.ds(pl.multiple_of(z * cap_z, cap_z), cap_z)

    def send_along_z(c):
        await_bytes(a_recv.at[c], a_rsem.at[c])
        b_send[c] = tn_dot(moves[...], a_recv[c]).astype(BF)
        pltpu.make_async_copy(b_send.at[c, line], out_ref.at[c, line], b_rsem.at[c]).start()

        @pl.loop(1, nz)
        def _(k):
            zz = lax.rem(z + k, nz)
            pltpu.make_async_remote_copy(
                src_ref=b_send.at[c, pl.ds(pl.multiple_of(zz * cap_z, cap_z), cap_z)], dst_ref=out_ref.at[c, line],
                send_sem=b_ssem.at[c], recv_sem=b_rsem.at[c],
                device_id=(zz * NX + x, trk), device_id_type=MESH).start()

    for c in range(chunks):
        attend(c)
        send_in_plane(c)
        if c == 0:
            lane = iota((per, nz * cap_z), 1).astype(F32)
            for v in range(npl):
                moves[v * per : (v + 1) * per, :] = jnp.where(target_ref[:, v : v + 1] == lane, 1.0, 0.0).astype(BF)
        else:
            send_along_z(c - 1)
    send_along_z(chunks - 1)
    for c in range(chunks):
        await_bytes(a_send.at[c, pl.ds(0, (npl - 1) * per)], a_ssem.at[c])
        await_bytes(b_send.at[c, pl.ds(0, (nz - 1) * cap_z)], b_ssem.at[c])
        await_bytes(out_ref.at[c], b_rsem.at[c])


def track_kernel(
    chunks,
    back_ref, slot_ref, embed_ref, gain_ref, valid_ref, keys_ref, scale_ref,
    wt_ref, wm_ref, bgain_ref, wh_ref, bh_ref, wb_ref,
    refined_ref, box_ref,
    projected, mixed,
):
    rows, width = embed_ref.shape
    entries = slot_ref.shape[0]
    listing = entries // rows
    slots = back_ref.shape[1]
    pick = jnp.where(slot_ref[...] == iota((entries, slots), 1), 1.0, 0.0).astype(BF)
    attended = jnp.concatenate(
        [jnp.dot(pick, back_ref[c], preferred_element_type=F32) for c in range(chunks)], axis=1)
    states = layer_norm(embed_ref[...].astype(F32)) * gain_ref[...]
    states = jnp.broadcast_to(states[:, None, :], (rows, listing, width)).reshape(entries, width)
    residual = states + attended
    normed = layer_norm(residual).astype(BF)
    projected[...] = jnp.dot(normed, wt_ref[...], preferred_element_type=F32).astype(BF)
    block = 128
    head = width // HEADS
    same = iota((block, block), 0) // listing == iota((block, block), 1) // listing
    for b in range(entries // block):
        at = slice(b * block, (b + 1) * block)
        open_keys = same & (keys_ref[:, at] > 0.5)
        for h in range(HEADS):
            q = projected[at, h * head : (h + 1) * head]
            k = projected[at, width + h * head : width + (h + 1) * head]
            v = projected[at, 2 * width + h * head : 2 * width + (h + 1) * head]
            scores = nt_dot(q, k) * (scale_ref[0, h] * head ** (-0.5))
            scores = jnp.where(open_keys, scores, MASKED)
            weights = jnp.exp(scores - jnp.max(scores, axis=-1, keepdims=True))
            probs = (weights / jnp.sum(weights, axis=-1, keepdims=True)).astype(BF)
            mixed[at, h * head : (h + 1) * head] = jnp.dot(probs, v, preferred_element_type=F32).astype(BF)
    updated = residual + jnp.dot(mixed[...], wm_ref[...], preferred_element_type=F32)
    valid = valid_ref[...]
    refined_ref[...] = (updated * valid).astype(BF)
    box_input = (layer_norm(updated) * bgain_ref[...]).astype(BF)
    hidden = jax.nn.gelu(jnp.dot(box_input, wh_ref[...], preferred_element_type=F32) + bh_ref[...]).astype(BF)
    box_ref[...] = jnp.dot(hidden, wb_ref[...], preferred_element_type=F32) * valid


def local(
    track_embed, view_ids, view_count, key_feats, value_feats, track_gain, w_temporal,
    temporal_scale, w_merge, box_gain, w_hidden, b_hidden, w_box,
):
    tm_count = lax.axis_size("tm")
    nt = lax.axis_size("trk")
    nz = tm_count // NX
    npl = NX * nt
    rows, width = track_embed.shape
    listing = view_ids.shape[1]
    entries = rows * listing
    tokens = key_feats.shape[2]
    per = nz * CAP
    total = npl * per
    cap_z = npl * CAP
    pair = 2
    chunks = HEADS // pair
    z = lax.axis_index("tm") // NX

    valid = jnp.arange(listing, dtype=jnp.int32)[None, :] < view_count[:, None]
    shown = jnp.where(valid, view_ids, -1)
    turned = jnp.tile(shown.T, (1, nz))
    lane = jnp.arange(nz * rows, dtype=jnp.int32)[None, :]
    turned = jnp.where(lane // rows == z, turned, -1)
    codes = time_code(z * NX + jnp.arange(NX, dtype=jnp.int32), width)
    flat = (shown * rows + jnp.arange(rows, dtype=jnp.int32)[:, None]).reshape(entries)
    plane = flat // (npl * rows)
    ahead = (flat[None, :] < flat[:, None]) & (flat[None, :] >= (plane * (npl * rows))[:, None])
    slot = plane * cap_z + jnp.sum(ahead.astype(jnp.int32), axis=1)
    slot = jnp.where(valid.reshape(entries), slot, -1)[:, None]

    anywhere = pl.BlockSpec(memory_space=pl.ANY)
    vmem = pl.BlockSpec(memory_space=pltpu.VMEM)
    dma = pltpu.SemaphoreType.DMA
    gain = track_gain[None, :]
    keys = key_feats.reshape(tokens, width)
    values = value_feats.reshape(tokens, width)
    arrived, next_keys, next_values, target = pl.pallas_call(
        functools.partial(forward_kernel, nz, nt, rows, cap_z),
        out_shape=(
            jax.ShapeDtypeStruct((total, width), BF),
            jax.ShapeDtypeStruct((tokens, width), BF),
            jax.ShapeDtypeStruct((tokens, width), BF),
            jax.ShapeDtypeStruct((per, npl), F32),
        ),
        in_specs=[vmem, vmem, vmem, vmem, anywhere, anywhere],
        out_specs=(anywhere, anywhere, anywhere, vmem),
        scratch_shapes=[
            pltpu.VMEM((nz, rows, width), BF),
            pltpu.VMEM((nz, listing, nz * rows), jnp.int32),
            pltpu.VMEM((total, width), BF),
            dma, dma, dma, dma, dma((2,)), dma((2,)), dma, dma, dma,
        ],
        compiler_params=pltpu.CompilerParams(
            collective_id=0, has_side_effects=True, vmem_limit_bytes=40 * 1024 * 1024),
        name="forward",
    )(track_embed, turned, codes, gain, keys, values)

    back = pl.pallas_call(
        functools.partial(return_kernel, nz, nt, cap_z, pair),
        out_shape=jax.ShapeDtypeStruct((chunks, nz * cap_z, pair * 128), BF),
        in_specs=[vmem] * 6,
        out_specs=anywhere,
        scratch_shapes=[
            pltpu.VMEM((chunks, total, pair * 128), BF),
            pltpu.VMEM((chunks, total, pair * 128), BF),
            pltpu.VMEM((total, nz * cap_z), BF),
            pltpu.VMEM((chunks, nz * cap_z, pair * 128), BF),
            dma((chunks,)), dma((chunks,)), dma((chunks,)), dma((chunks,)),
        ],
        compiler_params=pltpu.CompilerParams(
            collective_id=1, has_side_effects=True, vmem_limit_bytes=48 * 1024 * 1024),
        name="attend_and_return",
    )(arrived, keys, next_keys, values, next_values, target)

    seen = valid.astype(F32)
    boxes_wide = w_box.shape[1]
    refined, boxes = pl.pallas_call(
        functools.partial(track_kernel, chunks),
        out_shape=(
            jax.ShapeDtypeStruct((entries, width), BF),
            jax.ShapeDtypeStruct((entries, boxes_wide), F32),
        ),
        in_specs=[vmem] * 6 + [pl.BlockSpec(memory_space=pltpu.SMEM)] + [vmem] * 6,
        out_specs=(vmem, vmem),
        scratch_shapes=[pltpu.VMEM((entries, 3 * width), BF), pltpu.VMEM((entries, width), BF)],
        compiler_params=pltpu.CompilerParams(vmem_limit_bytes=56 * 1024 * 1024),
        name="track",
    )(
        back, slot, track_embed, gain, seen.reshape(entries, 1), seen.reshape(1, entries), temporal_scale[None, :],
        w_temporal, w_merge, box_gain[None, :], w_hidden, b_hidden[None, :], w_box,
    )
    return refined.reshape(rows, listing, width), boxes.reshape(rows, listing, boxes_wide)


def solution(mesh):
    placed = (
        P(("tm", "trk"), None),
        P(("tm", "trk"), None),
        P(("tm", "trk")),
        P("tm", "trk", None, None),
        P("tm", "trk", None, None),
    ) + (P(),) * 8
    return jax.shard_map(
        local,
        mesh=mesh,
        in_specs=placed,
        out_specs=(P(("tm", "trk"), None, None), P(("tm", "trk"), None, None)),
        check_vma=False,
    )
```

time: 253 us -> 172 us (0.68)
  Pallas kernels: 0 us -> 155 us
  waiting for transfers between devices: 93.6 us -> 0 us
  matrix products: 46 us -> 0 us
  local copies, waits for them, and re-layouts: 47.7 us -> 10.4 us
  starting transfers between devices: 29.4 us -> 0 us
  other arithmetic: 26.8 us -> 2.15 us
  loops' own time: 5.36 us -> 0 us
    pallas_call x0 -> x3, Pallas kernels: none -> 155 us  [the longest x1 77 us: local(): pl.pallas_call(functools.partial(return_kernel, nz, nt, cap_z, pair), out...]
    all_to_all x2 -> x0, waiting for transfers between devices: 54.4 us -> none  [one_exchange(): lax.all_to_all(blocks, axis, split_axis=0, concat_axis=0, tiled=True)]
    dot_general x20 -> x0, matrix products: 41.9 us -> none  [the longest x8 14.6 us: one_head(): jnp.einsum('slcd,lpd->lscp', query_part, key_part, preferred_element_type...]
    ppermute x2 -> x0, waiting for transfers between devices: 39.2 us -> none  [from_behind(): return lax.ppermute(block, axis, route)]
    all_to_all x2 -> x0, starting transfers between devices: 26.4 us -> none  [one_exchange(): lax.all_to_all(blocks, axis, split_axis=0, concat_axis=0, tiled=True)]
    reduce_sum x14 -> x1, other arithmetic: 13.6 us -> 0.35 us  [local(): slot = plane * cap_z + jnp.sum(ahead.astype(jnp.int32), axis=1)]
    another operation x3 -> x2, local copies, waits for them, and re-layouts: 12.6 us -> 0.09 us  [local(): turned = jnp.tile(shown.T, (1, nz))]
    dynamic_update_slice x16 -> x0, local copies, waits for them, and re-layouts: 6.97 us -> none  [attend_views(): per_head = lax.map(one_head, jnp.arange(HEADS, dtype=jnp.int32))]
  transfers between devices with their start and end apart: 4 -> 0, of which waited for: 4 -> 0; matrix products, arithmetic and copies ran while one was open for 2% -> 0% of each run, Pallas kernels for 0% -> 0%
where the time goes in v1:
time: 172 us; the launch traced here: 168 us
  Pallas kernels  155 us (90%)
  local copies, waits for them, and re-layouts  10.4 us (6%)
  other arithmetic  2.15 us (1%)
    pallas_call x1, Pallas kernels, local(): pl.pallas_call(functools.partial(return_kernel, nz, nt, cap_z, pair), out...  77 us
    pallas_call x1, Pallas kernels, local(): pl.pallas_call(functools.partial(forward_kernel, nz, nt, rows, cap_z), ou...  55.2 us
    pallas_call x1, Pallas kernels, local(): pl.pallas_call(functools.partial(track_kernel, chunks), out_shape=(jax.Sh...  22.8 us
    unnamed x20, local copies, waits for them, and re-layouts  7.84 us

profile of v1, /device:TPU:33, one launch (start us, length us, event | category | flops | bytes accessed | tf_op | source)
XLA Modules:
  0.0 168.3 jit_solution(5920601772760382056)
XLA Ops:
  0.7 0.1 multiply_sine_fusion
  0.8 0.7 iota_add_fusion
  1.6 0.1 tile.10
  1.7 0.0 copy-start
  1.7 1.2 copy-done
  2.9 0.0 copy-start.2
  2.9 1.2 copy-done.2
  4.1 0.8 copy-done.5
  5.0 0.7 copy-done.6
  5.6 55.2 %forward.1 = (bf16[1024,1024]{1,0:T(8,128)(2,1)S(1)}, bf16[512,1024]{1,0:T(8,128)(2,1)S(1)}, bf16[512,1024]{1,0:T(8,128)(2,1)S(1)}, f32[32,32]{1,0:T(8,128)S(1)}) custom-call(bf16[32,1024]{1,0:T(8,128)(2,1)S(1)} %copy-done.5, s32[16,256]{1,0:T(8,128)S(1)} %broadcast_select_fusion.ids_ref, f32[4,1024]{1,0:T(4,128)S(1)} %pad_maximum_fusion.code_ref, ...), custom_call_target="tpu_custom_call" | custom-call | tf_op jit(solution)/shard_map/forward/pallas_call | solution.py:345
  60.9 0.0 copy-start.4
  60.9 1.3 copy-done.4
  62.2 0.0 copy-done.1
  62.2 0.0 copy-done.3
  62.2 77.0 %attend_and_return.1.back_ref = bf16[4,1024,256]{2,1,0:T(8,128)(2,1)} custom-call(bf16[1024,1024]{1,0:T(8,128)(2,1)} %copy-done.4, bf16[512,1024]{1,0:T(8,128)(2,1)S(1)} %bitcast.12, bf16[512,1024]{1,0:T(8,128)(2,1)S(1)} %get-tuple-element.9.kn_ref, bf16[512,1024]{1,0:T(8,128)(2,1)S(1)} %bitcast.14, bf16[512,1024]{1,0:T(8,128)(2,1)S(1)} %get-tuple-element.10.vn_ref, ...), custom_call_target="tpu_custom_call" | custom-call | tf_op jit(solution)/shard_map/attend_and_return/pallas_call | solution.py:366
  139.3 0.1 copy.47
  139.3 0.1 lt.55
  139.4 0.4 convert_reduce_fusion
  139.8 0.2 copy.53
  139.9 0.2 reshape.240
  140.1 0.0 copy-done.8
  140.1 0.1 copy.46
  140.2 0.1 lt.54
  140.3 0.2 copy.54
  140.5 0.9 fusion.3.slot_ref
  141.4 0.9 copy.56.valid_ref
  142.3 0.1 copy.55
  142.3 0.7 reshape.239.keys_ref
  143.0 0.0 copy-done.7
  143.0 0.8 copy.57.wb_ref
  143.8 22.8 %track.1 = (bf16[512,1024]{1,0:T(8,128)(2,1)}, f32[512,10]{1,0:T(8,128)}) custom-call(bf16[4,1024,256]{2,1,0:T(8,128)(2,1)} %attend_and_return.1.back_ref, s32[512,1]{1,0:T(8,128)} %fusion.3.slot_ref, bf16[32,1024]{1,0:T(8,128)(2,1)} %embed_ref.3, f32[1,1024]{1,0:T(1,128)} %bitcast.15, f32[512,1]{1,0:T(8,128)} %copy.56.valid_ref, ...), custom_call_target="tpu_custom_call" | custom-call | tf_op jit(solution)/shard_map/track/pallas_call | solution.py:385
  166.6 1.8 %copy.58 = f32[32,16,10]{0,1,2:T(8,128)} copy(f32[32,16,10]{2,1,0:T(8,128)} %bitcast.17) | data formatting | bytes 40960
  (15 shorter events, 0.1 us)
Async XLA Ops:
  1.7 1.2 copy-start
  2.9 1.2 copy-start.2
  4.1 0.8 copy-start.5
  5.0 0.7 copy-start.6
  5.6 56.6 %copy-start.1 = (bf16[1,1,512,1024]{3,2,1,0:T(8,128)(2,1)S(1)}, bf16[1,1,512,1024]{3,2,1,0:T(8,128)(2,1)}, u32[]{:S(2)}) copy-start(bf16[1,1,512,1024]{3,2,1,0:T(8,128)(2,1)} %param.16) | copy-start | bytes 3145732
  5.6 56.6 %copy-start.3 = (bf16[1,1,512,1024]{3,2,1,0:T(8,128)(2,1)S(1)}, bf16[1,1,512,1024]{3,2,1,0:T(8,128)(2,1)}, u32[]{:S(2)}) copy-start(bf16[1,1,512,1024]{3,2,1,0:T(8,128)(2,1)} %param.17) | copy-start | bytes 3145732
  60.9 1.3 copy-start.4
  62.2 77.9 %copy-start.8 = (s32[32]{0:T(128)S(1)}, s32[32]{0:T(128)}, u32[]{:S(2)}) copy-start(s32[32]{0:T(128)} %param.15) | copy-start | bytes 388
  62.2 80.8 %copy-start.7 = (bf16[512,10]{0,1:T(8,128)(2,1)S(1)}, bf16[512,10]{0,1:T(8,128)(2,1)}, u32[]{:S(2)}) copy-start(bf16[512,10]{0,1:T(8,128)(2,1)} %param.25) | copy-start | bytes 30724

commit v2 on v1

v2 whole, which is shorter than its diff:
```python
import functools
import math

import jax
import jax.numpy as jnp
from jax import lax
from jax.experimental import pallas as pl
from jax.experimental.pallas import tpu as pltpu
from jax.sharding import PartitionSpec as P

HEADS = 8
CAMS = 8
CAP = 4
NX = 4
EPS = 1e-05
MASKED = -1e30
MESH = pl.DeviceIdType.MESH
BF = jnp.bfloat16
F32 = jnp.float32


def layer_norm(values):
    centre = jnp.mean(values, axis=-1, keepdims=True)
    shifted = values - centre
    spread = jnp.mean(shifted * shifted, axis=-1, keepdims=True)
    return shifted * lax.rsqrt(spread + EPS)


def time_code(frame_ids, model_width):
    half_width = model_width // 2
    freq_index = jnp.arange(half_width).astype(F32)
    freq_rates = jnp.exp(freq_index * (-2.0 * math.log(10000.0) / model_width))
    angles = frame_ids.astype(F32)[..., None] * freq_rates
    return jnp.concatenate([jnp.sin(angles), jnp.cos(angles)], axis=-1)


def iota(shape, dim):
    return lax.broadcasted_iota(jnp.int32, shape, dim)


def nt_dot(a, b):
    return lax.dot_general(a, b, (((1,), (1,)), ((), ())), preferred_element_type=F32)


def tn_dot(a, b):
    return lax.dot_general(a, b, (((0,), (0,)), ((), ())), preferred_element_type=F32)


def place(nt):
    tm = lax.axis_index("tm")
    trk = lax.axis_index("trk")
    z = tm // NX
    x = tm % NX
    return z, x, trk, x * nt + trk


def greet(nz, nt):
    z, x, trk, me = place(nt)
    npl = NX * nt
    barrier = pltpu.get_barrier_semaphore()

    @pl.loop(1, npl)
    def _(k):
        p = lax.rem(me + k, npl)
        pl.semaphore_signal(barrier, inc=1, device_id=(z * NX + p // nt, p % nt), device_id_type=MESH)

    @pl.loop(1, nz)
    def _(k):
        zz = lax.rem(z + k, nz)
        pl.semaphore_signal(barrier, inc=1, device_id=(zz * NX + x, trk), device_id_type=MESH)

    pl.semaphore_wait(barrier, npl - 1 + nz - 1)


def await_bytes(like, sem):
    pltpu.make_async_copy(like, like, sem).wait()


def z_order(nz):
    near = [0]
    for k in range(1, nz // 2 + 1):
        near += [k] if 2 * k == nz else [k, nz - k]
    return near


def mega_kernel(
    nz, nt, rows, cap, chunks, block,
    embed_ref, ids_ref, code_ref, gain_ref, key_ref, value_ref,
    back_ref, kept_ref, target_ref, most_ref,
    emb_z, ids_z, q_send, q_recv, kn_ref, vn_ref, a_send, a_recv, moves, b_send, most_one, most_all,
    z_send, z_recv, zi_send, zi_recv, kv_send, kv_recv, q_ssem, q_rsem, a_ssem, a_rsem, b_ssem, b_rsem,
    most_ssem, most_rsem, keep_sem,
):
    z, x, trk, me = place(nt)
    npl = NX * nt
    width = embed_ref.shape[1]
    order = z_order(nz)
    half = nz // 2
    per = half * CAP
    gcols = half * rows
    cols = nz * rows
    grows = npl * per
    head = 128
    wide = width // chunks
    scale = head ** (-0.5) * math.log2(math.e)
    listing = ids_ref.shape[0] - 8
    mine = pl.ds(pl.multiple_of(me * per, per), per)
    line = pl.ds(pl.multiple_of(z * cap, cap), cap)
    greet(nz, nt)

    def part(p):
        return pl.ds(pl.multiple_of(p * per, per), per)

    def in_plane(copy_to):
        @pl.loop(1, npl)
        def _(k):
            p = lax.rem(me + k, npl)
            copy_to(p, (z * NX + lax.div(p, nt), lax.rem(p, nt)))

    own_e = pltpu.make_async_copy(embed_ref, emb_z.at[0], z_recv.at[0])
    own_e.start()
    own_i = pltpu.make_async_copy(ids_ref, ids_z.at[0], zi_recv)
    own_i.start()
    for k in order[1:]:
        to = (lax.rem(z + k, nz) * NX + x, trk)
        pltpu.make_async_remote_copy(
            src_ref=ids_ref, dst_ref=ids_z.at[order.index(nz - k)], send_sem=zi_send, recv_sem=zi_recv,
            device_id=to, device_id_type=MESH).start()
    for k in order[1:]:
        to = (lax.rem(z + k, nz) * NX + x, trk)
        i = order.index(nz - k)
        pltpu.make_async_remote_copy(
            src_ref=embed_ref, dst_ref=emb_z.at[i], send_sem=z_send, recv_sem=z_recv.at[i],
            device_id=to, device_id_type=MESH).start()

    before = (z * NX + x, lax.rem(trk + nt - 1, nt))
    k_copy = pltpu.make_async_remote_copy(
        src_ref=key_ref, dst_ref=kn_ref, send_sem=kv_send.at[0], recv_sem=kv_recv.at[0],
        device_id=before, device_id_type=MESH)
    v_copy = pltpu.make_async_remote_copy(
        src_ref=value_ref, dst_ref=vn_ref, send_sem=kv_send.at[1], recv_sem=kv_recv.at[1],
        device_id=before, device_id_type=MESH)
    k_copy.start()
    v_copy.start()

    await_bytes(ids_z, zi_recv)
    lane = iota((listing, cols), 1) // rows
    ids = ids_z[0, :listing, :]
    most = ids_z[0, listing:, :128]
    for i in range(1, nz):
        ids = jnp.where(lane == i, ids_z[i, :listing, :], ids)
        most = jnp.maximum(most, ids_z[i, listing:, :128])
    most_one[...] = most
    pltpu.make_async_copy(most_one, most_all.at[me], most_rsem).start()
    in_plane(lambda p, to: pltpu.make_async_remote_copy(
        src_ref=most_one, dst_ref=most_all.at[me], send_sem=most_ssem, recv_sem=most_rsem,
        device_id=to, device_id_type=MESH).start())

    view = z * npl + iota((npl, cols), 0)
    named = jnp.zeros((npl, cols), F32)
    for j in range(listing):
        named = jnp.where(ids[j : j + 1, :] == view, 1.0, named)
    named_b = named.astype(BF)
    c0 = iota((cols, cols), 0)
    c1 = iota((cols, cols), 1)
    earlier = jnp.where((c0 < c1) & (c0 // rows == c1 // rows), 1.0, 0.0).astype(BF)
    rank = jnp.dot(named_b, earlier, preferred_element_type=F32)
    ranked = jnp.where(named > 0.5, rank, -1.0)

    same_z = iota((per, gcols), 0) // CAP == iota((per, gcols), 1) // rows
    slot_r = (iota((per, gcols), 0) % CAP).astype(F32)
    v0 = iota((npl, npl), 0)
    v1 = iota((npl, npl), 1)
    before_v = jnp.where(v0 < v1, 1.0, 0.0).astype(BF)
    t0 = iota((per, npl), 0)
    tr = (t0 % CAP).astype(F32)
    for g in range(2):
        counts = nt_dot(jnp.where(same_z, 1.0, 0.0).astype(BF), named_b[:, g * gcols : (g + 1) * gcols])
        base = jnp.dot(counts.astype(BF), before_v, preferred_element_type=F32)
        target_ref[g] = jnp.where(tr < counts, base + tr, -1.0)

    for g in range(2):
        for i in range(g * half, (g + 1) * half):
            await_bytes(emb_z.at[i], z_recv.at[i])
        states = emb_z[g * half : (g + 1) * half].reshape(gcols, width).astype(F32)
        states = layer_norm(states) * gain_ref[...]
        high = states.astype(BF)
        rest = states - high.astype(F32)
        middle = rest.astype(BF)
        low = (rest - middle.astype(F32)).astype(BF)
        parts = jnp.concatenate([high, middle, low], axis=0)
        picks = []
        for v in range(npl):
            here = ranked[v : v + 1, g * gcols : (g + 1) * gcols]
            picks.append(jnp.where(same_z & (here == slot_r), 1.0, 0.0).astype(BF))
        pick = jnp.concatenate(picks, axis=0)
        pick = jnp.concatenate([pick, pick, pick], axis=1)
        made = jnp.dot(pick, parts, preferred_element_type=F32)
        frow = grows // NX
        for f in range(NX):
            at = slice(f * frow, (f + 1) * frow)
            q_send[g, at] = (made[at] + code_ref[f : f + 1, :]).astype(BF)
        pltpu.make_async_copy(q_send.at[g, mine], q_recv.at[g, mine], q_rsem.at[g]).start()
        in_plane(lambda p, to: pltpu.make_async_remote_copy(
            src_ref=q_send.at[g, part(p)], dst_ref=q_recv.at[g, mine],
            send_sem=q_ssem.at[g], recv_sem=q_rsem.at[g], device_id=to, device_id_type=MESH).start())

    def attend(g, c):
        @pl.loop(0, grows // block)
        def _(b):
            at = pl.ds(pl.multiple_of(b * block, block), block)
            for h in range(wide // head):
                lanes = slice(c * wide + h * head, c * wide + (h + 1) * head)
                q = q_recv[g, at, lanes]
                s0 = nt_dot(q, key_ref[:, lanes])
                s1 = nt_dot(q, kn_ref[:, lanes])
                top = jnp.maximum(jnp.max(s0, axis=-1, keepdims=True), jnp.max(s1, axis=-1, keepdims=True))
                w0 = jnp.exp2((s0 - top) * scale)
                w1 = jnp.exp2((s1 - top) * scale)
                sums = jnp.sum(w0, axis=-1, keepdims=True) + jnp.sum(w1, axis=-1, keepdims=True)
                o = jnp.dot(w0.astype(BF), value_ref[:, lanes], preferred_element_type=F32)
                o = o + jnp.dot(w1.astype(BF), vn_ref[:, lanes], preferred_element_type=F32)
                a_send[g * chunks + c, at, h * head : (h + 1) * head] = (o / sums).astype(BF)

    def send_in_plane(n):
        pltpu.make_async_copy(a_send.at[n, mine], a_recv.at[n, mine], a_rsem.at[n]).start()
        in_plane(lambda p, to: pltpu.make_async_remote_copy(
            src_ref=a_send.at[n, part(p)], dst_ref=a_recv.at[n, mine],
            send_sem=a_ssem.at[n], recv_sem=a_rsem.at[n], device_id=to, device_id_type=MESH).start())

    def send_along_z(n):
        g, c = n // chunks, n % chunks
        await_bytes(a_recv.at[n], a_rsem.at[n])
        pltpu.make_async_copy(a_recv.at[n], kept_ref.at[n], keep_sem.at[n]).start()
        b_send[n] = tn_dot(moves[g], a_recv[n]).astype(BF)
        for i in range(half):
            dz = order[g * half + i]
            src = b_send.at[n, pl.ds(i * cap, cap)]
            if dz == 0:
                pltpu.make_async_copy(src, back_ref.at[c, line], b_rsem.at[n]).start()
            else:
                pltpu.make_async_remote_copy(
                    src_ref=src, dst_ref=back_ref.at[c, line], send_sem=b_ssem.at[n], recv_sem=b_rsem.at[n],
                    device_id=(lax.rem(z + dz, nz) * NX + x, trk), device_id_type=MESH).start()

    k_copy.wait()
    v_copy.wait()
    for n in range(2 * chunks):
        g, c = n // chunks, n % chunks
        if c == 0:
            await_bytes(q_recv.at[g], q_rsem.at[g])
        attend(g, c)
        send_in_plane(n)
        if n == 0:
            goal = iota((per, half * cap), 1)
            goal_z = iota((per, half * cap), 0) // CAP == goal // cap
            goal_at = (goal % cap).astype(F32)
            for gg in range(2):
                for v in range(npl):
                    hit = goal_z & (target_ref[gg, :, v : v + 1] == goal_at)
                    moves[gg, v * per : (v + 1) * per, :] = jnp.where(hit, 1.0, 0.0).astype(BF)
        else:
            send_along_z(n - 1)
    send_along_z(2 * chunks - 1)

    await_bytes(emb_z.at[pl.ds(0, nz - 1)], z_send)
    await_bytes(ids_z.at[pl.ds(0, nz - 1)], zi_send)
    await_bytes(most_all.at[pl.ds(0, npl - 1)], most_ssem)
    await_bytes(most_all, most_rsem)
    most_ref[...] = jnp.max(most_all[...], axis=0)
    for g in range(2):
        await_bytes(q_send.at[g, pl.ds(0, (npl - 1) * per)], q_ssem.at[g])
    for n in range(2 * chunks):
        remote = sum(1 for i in range(half) if order[n // chunks * half + i] != 0)
        await_bytes(a_send.at[n, pl.ds(0, (npl - 1) * per)], a_ssem.at[n])
        await_bytes(b_send.at[n, pl.ds(0, remote * cap)], b_ssem.at[n])
        await_bytes(back_ref.at[0, pl.ds(0, half * cap)], b_rsem.at[n])
        await_bytes(kept_ref.at[n], keep_sem.at[n])


def rest_kernel(
    nz, nt, cap, chunks,
    kept_ref, target_ref,
    back_ref,
    kept, moves, b_send, load_sem, b_ssem, b_rsem,
):
    z, x, trk, me = place(nt)
    npl = NX * nt
    order = z_order(nz)
    half = nz // 2
    per = half * CAP
    line = pl.ds(pl.multiple_of(z * cap, cap), cap)
    greet(nz, nt)
    load = pltpu.make_async_copy(kept_ref, kept, load_sem)
    load.start()
    load.wait()
    goal = iota((per, half * cap), 1)
    goal_z = iota((per, half * cap), 0) // CAP == goal // cap
    goal_at = (goal % cap + cap).astype(F32)
    for g in range(2):
        for v in range(npl):
            hit = goal_z & (target_ref[g, :, v : v + 1] == goal_at)
            moves[g, v * per : (v + 1) * per, :] = jnp.where(hit, 1.0, 0.0).astype(BF)
    for n in range(2 * chunks):
        g, c = n // chunks, n % chunks
        b_send[n] = tn_dot(moves[g], kept[n]).astype(BF)
        for i in range(half):
            dz = order[g * half + i]
            src = b_send.at[n, pl.ds(i * cap, cap)]
            if dz == 0:
                pltpu.make_async_copy(src, back_ref.at[c, line], b_rsem.at[n]).start()
            else:
                pltpu.make_async_remote_copy(
                    src_ref=src, dst_ref=back_ref.at[c, line], send_sem=b_ssem.at[n], recv_sem=b_rsem.at[n],
                    device_id=(lax.rem(z + dz, nz) * NX + x, trk), device_id_type=MESH).start()
    for n in range(2 * chunks):
        remote = sum(1 for i in range(half) if order[n // chunks * half + i] != 0)
        await_bytes(b_send.at[n, pl.ds(0, remote * cap)], b_ssem.at[n])
        await_bytes(back_ref.at[0, pl.ds(0, half * cap)], b_rsem.at[n])


def track_kernel(
    chunks, lists, cap, *refs,
):
    backs, refs = refs[:lists], refs[lists:]
    (
        slot_ref, embed_ref, gain_ref, valid_ref, keys_ref, scale_ref,
        wt_ref, wm_ref, bgain_ref, wh_ref, bh_ref, wb_ref,
        refined_ref, box_ref,
        projected, mixed,
    ) = refs
    rows, width = embed_ref.shape
    entries = slot_ref.shape[0]
    listing = entries // rows
    slots = backs[0].shape[1]
    column = iota((entries, slots), 1)
    attended = 0.0
    for k in range(lists):
        sought = (column // cap) * (CAP * NX * CAMS) + column % cap + k * cap
        pick = jnp.where(slot_ref[...] == sought, 1.0, 0.0).astype(BF)
        attended = attended + jnp.concatenate(
            [jnp.dot(pick, backs[k][c], preferred_element_type=F32) for c in range(chunks)], axis=1)
    states = layer_norm(embed_ref[...].astype(F32)) * gain_ref[...]
    states = jnp.broadcast_to(states[:, None, :], (rows, listing, width)).reshape(entries, width)
    residual = states + attended
    normed = layer_norm(residual).astype(BF)
    projected[...] = jnp.dot(normed, wt_ref[...], preferred_element_type=F32).astype(BF)
    block = 128
    head = width // HEADS
    same = iota((block, block), 0) // listing == iota((block, block), 1) // listing
    for b in range(entries // block):
        at = slice(b * block, (b + 1) * block)
        open_keys = same & (keys_ref[:, at] > 0.5)
        for h in range(HEADS):
            q = projected[at, h * head : (h + 1) * head]
            k = projected[at, width + h * head : width + (h + 1) * head]
            v = projected[at, 2 * width + h * head : 2 * width + (h + 1) * head]
            scores = nt_dot(q, k) * (scale_ref[0, h] * head ** (-0.5))
            scores = jnp.where(open_keys, scores, MASKED)
            weights = jnp.exp(scores - jnp.max(scores, axis=-1, keepdims=True))
            probs = (weights / jnp.sum(weights, axis=-1, keepdims=True)).astype(BF)
            mixed[at, h * head : (h + 1) * head] = jnp.dot(probs, v, preferred_element_type=F32).astype(BF)
    updated = residual + jnp.dot(mixed[...], wm_ref[...], preferred_element_type=F32)
    valid = valid_ref[...]
    refined_ref[...] = (updated * valid).astype(BF)
    box_input = (layer_norm(updated) * bgain_ref[...]).astype(BF)
    hidden = jax.nn.gelu(jnp.dot(box_input, wh_ref[...], preferred_element_type=F32) + bh_ref[...]).astype(BF)
    box_ref[...] = jnp.dot(hidden, wb_ref[...], preferred_element_type=F32) * valid


def local(
    track_embed, view_ids, view_count, key_feats, value_feats, track_gain, w_temporal,
    temporal_scale, w_merge, box_gain, w_hidden, b_hidden, w_box,
):
    tm_count = lax.axis_size("tm")
    nt = lax.axis_size("trk")
    nz = tm_count // NX
    npl = NX * nt
    rows, width = track_embed.shape
    listing = view_ids.shape[1]
    entries = rows * listing
    tokens = key_feats.shape[2]
    per = nz * CAP
    total = npl * per
    longest = npl * CAP
    cap = longest // 2
    chunks = 2
    z = lax.axis_index("tm") // NX

    valid = jnp.arange(listing, dtype=jnp.int32)[None, :] < view_count[:, None]
    shown = jnp.where(valid, view_ids, -1)
    codes = time_code(z * NX + jnp.arange(NX, dtype=jnp.int32), width)
    flat = (shown * rows + jnp.arange(rows, dtype=jnp.int32)[:, None]).reshape(entries)
    plane = flat // (npl * rows)
    ahead = (flat[None, :] < flat[:, None]) & (flat[None, :] >= (plane * (npl * rows))[:, None])
    slot = plane * longest + jnp.sum(ahead.astype(jnp.int32), axis=1)
    slot = jnp.where(valid.reshape(entries), slot, -1)[:, None]

    in_plane_of = jnp.arange(nz, dtype=jnp.int32)
    crowd = jnp.max(jnp.sum((plane[None, :] == in_plane_of[:, None]).astype(jnp.int32), axis=1))
    turned = jnp.concatenate(
        [jnp.tile(shown.T, (1, nz)), jnp.broadcast_to(crowd, (8, nz * rows))], axis=0)

    anywhere = pl.BlockSpec(memory_space=pl.ANY)
    vmem = pl.BlockSpec(memory_space=pltpu.VMEM)
    dma = pltpu.SemaphoreType.DMA
    gain = track_gain[None, :]
    keys = key_feats.reshape(tokens, width)
    values = value_feats.reshape(tokens, width)
    count = 2 * chunks
    wide = width // chunks
    per = nz // 2 * CAP
    grows = npl * per
    back, kept, target, most = pl.pallas_call(
        functools.partial(mega_kernel, nz, nt, rows, cap, chunks, 256),
        out_shape=(
            jax.ShapeDtypeStruct((chunks, nz * cap, wide), BF),
            jax.ShapeDtypeStruct((count, grows, wide), BF),
            jax.ShapeDtypeStruct((2, per, npl), F32),
            jax.ShapeDtypeStruct((8, 128), jnp.int32),
        ),
        in_specs=[vmem] * 6,
        out_specs=(anywhere, anywhere, vmem, vmem),
        scratch_shapes=[
            pltpu.VMEM((nz, rows, width), BF),
            pltpu.VMEM((nz, listing + 8, nz * rows), jnp.int32),
            pltpu.VMEM((2, grows, width), BF),
            pltpu.VMEM((2, grows, width), BF),
            pltpu.VMEM((tokens, width), BF),
            pltpu.VMEM((tokens, width), BF),
            pltpu.VMEM((count, grows, wide), BF),
            pltpu.VMEM((count, grows, wide), BF),
            pltpu.VMEM((2, grows, nz // 2 * cap), BF),
            pltpu.VMEM((count, nz // 2 * cap, wide), BF),
            pltpu.VMEM((8, 128), jnp.int32),
            pltpu.VMEM((npl, 8, 128), jnp.int32),
            dma, dma((nz,)), dma, dma, dma((2,)), dma((2,)), dma((2,)), dma((2,)),
            dma((count,)), dma((count,)), dma((count,)), dma((count,)), dma, dma, dma((count,)),
        ],
        compiler_params=pltpu.CompilerParams(
            collective_id=0, has_side_effects=True, vmem_limit_bytes=52 * 1024 * 1024),
        name="mega",
    )(track_embed, turned, codes, gain, keys, values)

    seen = valid.astype(F32)
    boxes_wide = w_box.shape[1]
    shared = (
        slot, track_embed, gain, seen.reshape(entries, 1), seen.reshape(1, entries), temporal_scale[None, :],
        w_temporal, w_merge, box_gain[None, :], w_hidden, b_hidden[None, :], w_box,
    )

    def finish(*backs):
        return pl.pallas_call(
            functools.partial(track_kernel, chunks, len(backs), cap),
            out_shape=(
                jax.ShapeDtypeStruct((entries, width), BF),
                jax.ShapeDtypeStruct((entries, boxes_wide), F32),
            ),
            in_specs=[vmem] * (len(backs) + 5) + [pl.BlockSpec(memory_space=pltpu.SMEM)] + [vmem] * 6,
            out_specs=(vmem, vmem),
            scratch_shapes=[pltpu.VMEM((entries, 3 * width), BF), pltpu.VMEM((entries, width), BF)],
            compiler_params=pltpu.CompilerParams(vmem_limit_bytes=56 * 1024 * 1024),
            name="track",
        )(*backs, *shared)

    def finish_long():
        rest = pl.pallas_call(
            functools.partial(rest_kernel, nz, nt, cap, chunks),
            out_shape=jax.ShapeDtypeStruct((chunks, nz * cap, wide), BF),
            in_specs=[anywhere, vmem],
            out_specs=anywhere,
            scratch_shapes=[
                pltpu.VMEM((count, grows, wide), BF),
                pltpu.VMEM((2, grows, nz // 2 * cap), BF),
                pltpu.VMEM((count, nz // 2 * cap, wide), BF),
                dma, dma((count,)), dma((count,)),
            ],
            compiler_params=pltpu.CompilerParams(
                collective_id=1, has_side_effects=True, vmem_limit_bytes=32 * 1024 * 1024),
            name="rest",
        )(kept, target)
        return finish(back, rest)

    refined, boxes = lax.cond(most[0, 0] > cap, finish_long, lambda: finish(back))
    return refined.reshape(rows, listing, width), boxes.reshape(rows, listing, boxes_wide)


def solution(mesh):
    placed = (
        P(("tm", "trk"), None),
        P(("tm", "trk"), None),
        P(("tm", "trk")),
        P("tm", "trk", None, None),
        P("tm", "trk", None, None),
    ) + (P(),) * 8
    return jax.shard_map(
        local,
        mesh=mesh,
        in_specs=placed,
        out_specs=(P(("tm", "trk"), None, None), P(("tm", "trk"), None, None)),
        check_vma=False,
    )
```

time: 172 us -> 143 us (0.83); the launches traced: 168 us -> 141 us
  Pallas kernels: 155 us -> 130 us
  local copies, waits for them, and re-layouts: 10.4 us -> 6.4 us
    pallas_call x3 -> x2, Pallas kernels: 155 us -> 130 us  [the longest x1 110 us: local(): pl.pallas_call(functools.partial(mega_kernel, nz, nt, rows, cap, chunks,...]
    unnamed x20 -> x17, local copies, waits for them, and re-layouts: 7.84 us -> 2.08 us
    another operation x2 -> x5, local copies, waits for them, and re-layouts: 0.09 us -> 2.59 us  [local(): turned = jnp.tile(shown.T, (1, nz))]
where the time goes in v2:
time: 143 us; the launch traced here: 141 us
  Pallas kernels  130 us (91%)
  local copies, waits for them, and re-layouts  6.4 us (4%)
  other arithmetic  2.68 us (2%)
  between operations  1.48 us (1%)
    pallas_call x1, Pallas kernels, local(): pl.pallas_call(functools.partial(mega_kernel, nz, nt, rows, cap, chunks,...  110 us
    pallas_call x1, Pallas kernels, finish(): pl.pallas_call(functools.partial(track_kernel, chunks, len(backs), cap),...  20.9 us

profile of v2, /device:TPU:33, one launch (start us, length us, event | category | flops | bytes accessed | tf_op | source)
XLA Modules:
  0.0 141.2 jit_solution(3651985745668268674)
XLA Ops:
  0.6 0.0 copy-start.4
  0.6 0.0 copy-start.5
  0.7 0.0 copy-start.8
  0.7 0.0 copy-start.7
  0.7 0.0 copy-start.9
  0.7 0.0 copy-start.6
  0.7 0.7 fusion
  1.4 0.1 copy.33
  1.5 0.1 lt.52
  1.6 0.1 copy.35
  1.7 0.1 reshape.244
  1.8 0.1 multiply_sine_fusion
  1.9 0.7 iota_add_fusion
  2.6 0.1 copy.32
  2.7 0.1 reshape.237
  2.8 0.1 reshape.240
  2.9 0.3 convert_reduce_fusion
  3.3 0.1 convert_reduce_fusion.1
  3.4 0.6 reduce_max.9
  4.0 0.1 tile.10
  4.1 0.7 concatenate.6.ids_ref
  4.8 0.0 copy-start.1
  4.8 1.2 copy-done.1
  6.0 109.5 %mega.1 = (bf16[2,512,512]{2,1,0:T(8,128)(2,1)}, bf16[4,512,512]{2,1,0:T(8,128)(2,1)}, f32[2,16,32]{2,1,0:T(8,128)S(1)}, s32[8,128]{1,0:T(8,128)S(1)}) custom-call(bf16[32,1024]{1,0:T(8,128)(2,1)} %embed_ref.1, s32[24,256]{1,0:T(8,128)S(1)} %concatenate.6.ids_ref, f32[4,1024]{1,0:T(4,128)S(1)} %pad_maximum_fusion.code_ref, f32[1,1024]{1,0:T(1,128)} %bitcast.15, ...), custom_call_target="tpu_custom_call" | custom-call | tf_op jit(solution)/shard_map/mega/pallas_call | solution.py:414
  115.6 0.5 slice.3
  116.7 0.0 copy-done.4
  116.8 23.6 %conditional.1 = ((bf16[512,1024]{1,0:T(8,128)(2,1)}, f32[512,10]{1,0:T(8,128)S(1)})) conditional(s32[]{:T(128)} %bitcast.4, (bf16[2,512,512]{2,1,0:T(8,128)(2,1)}, s32[512,1]{0,1:T(1,128)S(1)}, bf16[32,1024]{1,0:T(8,128)(2,1)S(1)}, f32[1,1024]{1,0:T(1,128)S(1)}, f32[512,1]{0,1:T(1,128)S(1)}, /*index=5*/f32[1,512]{1,0:T(1,128)S(1)}, ...), branch_computations={%region_3.4_spmd, %region_4.5_spmd} | conditional | bytes 8417344 | solution.py:484
  117.0 0.8 copy.38.refs_12_
  117.8 0.9 copy.37.refs_4_
  118.6 0.9 copy.36.refs_1_
  119.5 20.9 %track.2 = (bf16[512,1024]{1,0:T(8,128)(2,1)}, f32[512,10]{1,0:T(8,128)S(1)}) custom-call(bf16[2,512,512]{2,1,0:T(8,128)(2,1)} %get-tuple-element.62.refs_0_, s32[512,1]{1,0:T(8,128)} %copy.36.refs_1_, bf16[32,1024]{1,0:T(8,128)(2,1)S(1)} %get-tuple-element.64.refs_2_, f32[1,1024]{1,0:T(1,128)S(1)} %get-tuple-element.65.refs_3_, f32[512,1]{1,0:T(8,128)} %copy.37.refs_4_, ...), custom_call_target="tpu_custom_call" | custom-call | tf_op jit(solution)/shard_map/cond/branch_0_fun/track/pallas_call | solution.py:453
  140.4 0.8 copy.43
  (14 shorter events, 0.1 us)
Async XLA Ops:
  0.6 116.1 %copy-start.4 = (bf16[32,1024]{1,0:T(8,128)(2,1)S(1)}, bf16[32,1024]{1,0:T(8,128)(2,1)}, u32[]{:S(2)}) copy-start(bf16[32,1024]{1,0:T(8,128)(2,1)} %embed_ref.1) | copy-start | bytes 196612
  0.6 116.1 %copy-start.5 = (bf16[512,10]{0,1:T(8,128)(2,1)S(1)}, bf16[512,10]{0,1:T(8,128)(2,1)}, u32[]{:S(2)}) copy-start(bf16[512,10]{0,1:T(8,128)(2,1)} %param.27) | copy-start | bytes 30724
  0.7 116.1 %copy-start.8 = (f32[512]{0:T(512)S(1)}, f32[512]{0:T(512)}, u32[]{:S(2)}) copy-start(f32[512]{0:T(512)} %param.26) | copy-start | bytes 6148
  0.7 116.1 %copy-start.7 = (f32[1024]{0:T(1024)S(1)}, f32[1024]{0:T(1024)}, u32[]{:S(2)}) copy-start(f32[1024]{0:T(1024)} %param.24) | copy-start | bytes 12292
  0.7 116.1 %copy-start.9 = (f32[8]{0:T(128)S(1)}, f32[8]{0:T(128)}, u32[]{:S(2)}) copy-start(f32[8]{0:T(128)} %param.22) | copy-start | bytes 100
  0.7 116.1 %copy-start.6 = (f32[1024]{0:T(1024)S(1)}, f32[1024]{0:T(1024)}, u32[]{:S(2)}) copy-start(f32[1024]{0:T(1024)} %param.20) | copy-start | bytes 12292
  4.8 1.2 copy-start.1
  6.0 110.8 %copy-start.2 = (bf16[1024,1024]{1,0:T(8,128)(2,1)S(1)}, bf16[1024,1024]{1,0:T(8,128)(2,1)}, u32[]{:S(2)}) copy-start(bf16[1024,1024]{1,0:T(8,128)(2,1)} %param.23) | copy-start | bytes 6291460

commit v3 on v2

--- a/solution.py
+++ b/solution.py
@@ -11,6 +11,7 @@
 HEADS = 8
 CAMS = 8
 CAP = 4
+CORES = 2
 NX = 4
 EPS = 1e-05
 MASKED = -1e30
@@ -87,18 +88,23 @@
     nz, nt, rows, cap, chunks, block,
     embed_ref, ids_ref, code_ref, gain_ref, key_ref, value_ref,
     back_ref, kept_ref, target_ref, most_ref,
-    emb_z, ids_z, q_send, q_recv, kn_ref, vn_ref, a_send, a_recv, moves, b_send, most_one, most_all,
-    z_send, z_recv, zi_send, zi_recv, kv_send, kv_recv, q_ssem, q_rsem, a_ssem, a_rsem, b_ssem, b_rsem,
-    most_ssem, most_rsem, keep_sem,
+    emb_z, ids_y, ids_z, q_send, q_recv, kk_ref, vv_ref, a_send, a_recv, moves, b_send, most_one, most_all,
+    y_send, y_recv, yi_send, yi_recv, z_send, z_recv, zi_send, zi_recv, kv_own, kv_send, kv_recv,
+    q_ssem, q_rsem, a_ssem, a_rsem, b_ssem, b_rsem, most_ssem, most_rsem, keep_sem,
 ):
     z, x, trk, me = place(nt)
+    y, core = trk // CORES, trk % CORES
+    ny = nt // CORES
     npl = NX * nt
+    nx = NX * CORES
+    me_x = x * CORES + core
     width = embed_ref.shape[1]
+    tokens = key_ref.shape[0]
     order = z_order(nz)
     half = nz // 2
     per = half * CAP
-    gcols = half * rows
-    cols = nz * rows
+    lot = ny * per
+    lanes = ny * rows
     grows = npl * per
     head = 128
     wide = width // chunks
@@ -108,125 +114,193 @@
     line = pl.ds(pl.multiple_of(z * cap, cap), cap)
     greet(nz, nt)
 
-    def part(p):
-        return pl.ds(pl.multiple_of(p * per, per), per)
-
-    def in_plane(copy_to):
+    own_e = pltpu.make_async_copy(embed_ref, emb_z.at[0, 0], y_recv)
+    own_e.start()
+    own_i = pltpu.make_async_copy(ids_ref, ids_y.at[0], yi_recv)
+    own_i.start()
+    for k in range(1, ny):
+        to = (z * NX + x, lax.rem(y + k, ny) * CORES + core)
+        pltpu.make_async_remote_copy(
+            src_ref=ids_ref, dst_ref=ids_y.at[ny - k], send_sem=yi_send, recv_sem=yi_recv,
+            device_id=to, device_id_type=MESH).start()
+    for k in range(1, ny):
+        to = (z * NX + x, lax.rem(y + k, ny) * CORES + core)
+        pltpu.make_async_remote_copy(
+            src_ref=embed_ref, dst_ref=emb_z.at[0, ny - k], send_sem=y_send, recv_sem=y_recv,
+            device_id=to, device_id_type=MESH).start()
+
+    before = (z * NX + x, lax.rem(trk + nt - 1, nt))
+    first, second = pl.ds(0, tokens), pl.ds(tokens, tokens)
+    copies = []
+    for i, (own, both) in enumerate(((key_ref, kk_ref), (value_ref, vv_ref))):
+        copies.append(pltpu.make_async_copy(own, both.at[first], kv_own.at[i]))
+        copies.append(pltpu.make_async_remote_copy(
+            src_ref=own, dst_ref=both.at[second], send_sem=kv_send.at[i], recv_sem=kv_recv.at[i],
+            device_id=before, device_id_type=MESH))
+
+    await_bytes(ids_y, yi_recv)
+    lane = iota(ids_y.shape[1:], 1) // rows
+    ids = ids_y[0]
+    most = ids_y[0, listing:, :]
+    for i in range(1, ny):
+        ids = jnp.where(lane == i, ids_y[i], ids)
+        most = jnp.maximum(most, ids_y[i, listing:, :])
+    ids_z[0, :listing, :] = ids[:listing]
+    ids_z[0, listing:, :] = most
+    await_bytes(emb_z.at[0], y_recv)
+
+    def to_z(source, step, part=None):
+        target = (source - step) % nz
+        device = (lax.rem(z + nz + step, nz) * NX + x, trk)
+        if part is None or part == 0:
+            pltpu.make_async_remote_copy(
+                src_ref=ids_z.at[source], dst_ref=ids_z.at[target], send_sem=zi_send, recv_sem=zi_recv.at[target],
+                device_id=device, device_id_type=MESH).start()
+        src, dst = emb_z.at[source], emb_z.at[target]
+        if part is not None:
+            few = pl.ds(part * (ny // 2), ny // 2)
+            src, dst = emb_z.at[source, few], emb_z.at[target, few]
+        pltpu.make_async_remote_copy(
+            src_ref=src, dst_ref=dst, send_sem=z_send, recv_sem=z_recv.at[target],
+            device_id=device, device_id_type=MESH).start()
+
+    def arrive(slot):
+        await_bytes(ids_z.at[slot], zi_recv.at[slot])
+        await_bytes(emb_z.at[slot], z_recv.at[slot])
+
+    to_z(0, 1)
+    to_z(0, -1)
+    for copy in copies:
+        copy.start()
+
+    view_x = iota((nx, lanes), 0)
+    view_x = (z * NX + view_x // CORES) * nt + y * CORES + view_x % CORES
+    view_p = z * npl + iota((npl, lanes), 0)
+    c0 = iota((lanes, lanes), 0)
+    c1 = iota((lanes, lanes), 1)
+    earlier = jnp.where((c0 < c1) & (c0 // rows == c1 // rows), 1.0, 0.0).astype(BF)
+    lane_at = iota((nx, lanes), 1) // rows
+    slot_row = iota((per, lanes), 0)
+    same_z = slot_row // CAP == iota((per, lanes), 1) // rows
+    slot_r = (slot_row % CAP).astype(F32)
+    own_lane = iota((per, lanes), 1) < rows
+    v0 = iota((npl, npl), 0)
+    v1 = iota((npl, npl), 1)
+    before_v = jnp.where(v0 < v1, 1.0, 0.0).astype(BF)
+    tr = (iota((per, npl), 0) % CAP).astype(F32)
+
+    def names(ids, view):
+        named = jnp.zeros(view.shape, F32)
+        for j in range(listing):
+            named = jnp.where(ids[j : j + 1, :] == view, 1.0, named)
+        return named
+
+    def build(g):
+        slots = order[g * half : (g + 1) * half]
+        ranked, parts = [], []
+        counts = jnp.zeros((per, npl), F32)
+        for i, slot in enumerate(slots):
+            ids = ids_z[slot, :listing, :]
+            named = names(ids, view_x)
+            rank = jnp.dot(named.astype(BF), earlier, preferred_element_type=F32)
+            ranked.append(jnp.where(named > 0.5, rank, -1.0))
+            here = jnp.where((slot_row // CAP == i) & own_lane, 1.0, 0.0).astype(BF)
+            counts = counts + nt_dot(here, names(ids, view_p).astype(BF))
+            states = layer_norm(emb_z[slot].reshape(lanes, width).astype(F32)) * gain_ref[...]
+            high = states.astype(BF)
+            rest = states - high.astype(F32)
+            middle = rest.astype(BF)
+            low = (rest - middle.astype(F32)).astype(BF)
+            parts.append((high, middle, low))
+        base = jnp.dot(counts.astype(BF), before_v, preferred_element_type=F32)
+        target_ref[g] = jnp.where(tr < counts, base + tr, -1.0)
+        for dy in range(ny):
+            here = jnp.zeros((nx, lanes), F32)
+            for i in range(half):
+                shift = (i - dy) * rows % lanes
+                moved = pltpu.roll(ranked[i], shift, 1) if shift else ranked[i]
+                here = jnp.where(lane_at == i, moved, here)
+            picks = [jnp.where(same_z & (here[v : v + 1, :] == slot_r), 1.0, 0.0).astype(BF) for v in range(nx)]
+            pick = jnp.concatenate(picks, axis=0)
+            pick = jnp.concatenate([pick, pick, pick], axis=1)
+            at = slice(dy * rows, (dy + 1) * rows)
+            source = jnp.concatenate([parts[i][k][at] for k in range(3) for i in range(half)], axis=0)
+            made = jnp.dot(pick, source, preferred_element_type=F32)
+            for v in range(nx):
+                f = v // CORES
+                one = made[v * per : (v + 1) * per] + code_ref[f : f + 1, :]
+                q_send[g, v * lot + dy * per : v * lot + (dy + 1) * per, :] = one.astype(BF)
+        block_x = pl.ds(pl.multiple_of(me_x * lot, lot), lot)
+        pltpu.make_async_copy(q_send.at[g, block_x], q_recv.at[g, block_x], q_rsem.at[g]).start()
+        for k in range(1, nx):
+            p = lax.rem(me_x + k, nx)
+            pltpu.make_async_remote_copy(
+                src_ref=q_send.at[g, pl.ds(pl.multiple_of(p * lot, lot), lot)], dst_ref=q_recv.at[g, block_x],
+                send_sem=q_ssem.at[g], recv_sem=q_rsem.at[g],
+                device_id=(z * NX + lax.div(p, CORES), y * CORES + lax.rem(p, CORES)), device_id_type=MESH).start()
+
+    for k in range(1, half):
+        arrive(nz - k)
+        if k < half - 1:
+            to_z(nz - k, 1)
+        else:
+            to_z(nz - k, 1, 0)
+        arrive(k)
+        if k < half - 1:
+            to_z(k, -1)
+        else:
+            to_z(k, -1, 1)
+        if k == 2:
+            build(0)
+    arrive(half)
+    build(1)
+
+    most = ids_z[0, listing:, :]
+    for i in range(1, nz):
+        most = jnp.maximum(most, ids_z[i, listing:, :])
+    most_one[...] = most
+    pltpu.make_async_copy(most_one, most_all.at[me_x], most_rsem).start()
+    for k in range(1, nx):
+        p = lax.rem(me_x + k, nx)
+        pltpu.make_async_remote_copy(
+            src_ref=most_one, dst_ref=most_all.at[me_x], send_sem=most_ssem, recv_sem=most_rsem,
+            device_id=(z * NX + lax.div(p, CORES), y * CORES + lax.rem(p, CORES)), device_id_type=MESH).start()
+
+    def attend(g, c):
+        def score(at, h):
+            some = slice(c * wide + h * head, c * wide + (h + 1) * head)
+            return nt_dot(q_recv[g, at, some], kk_ref[:, some])
+
+        @pl.loop(0, grows // block)
+        def _(b):
+            at = pl.ds(pl.multiple_of(b * block, block), block)
+            ahead = score(at, 0)
+            for h in range(wide // head):
+                scores = ahead
+                if h + 1 < wide // head:
+                    ahead = score(at, h + 1)
+                top = jnp.max(scores, axis=-1, keepdims=True)
+                weights = jnp.exp2((scores - top) * scale)
+                sums = jnp.sum(weights, axis=-1, keepdims=True)
+                some = slice(c * wide + h * head, c * wide + (h + 1) * head)
+                o = jnp.dot(weights.astype(BF), vv_ref[:, some], preferred_element_type=F32)
+                a_send[g * chunks + c, at, h * head : (h + 1) * head] = (o / sums).astype(BF)
+
+    def rows_of(px, dy):
+        return pl.ds(pl.multiple_of(px * lot + dy * per, per), per)
+
+    def send_in_plane(n):
+        pltpu.make_async_copy(a_send.at[n, rows_of(me_x, 0)], a_recv.at[n, mine], a_rsem.at[n]).start()
+
         @pl.loop(1, npl)
         def _(k):
             p = lax.rem(me + k, npl)
-            copy_to(p, (z * NX + lax.div(p, nt), lax.rem(p, nt)))
-
-    own_e = pltpu.make_async_copy(embed_ref, emb_z.at[0], z_recv.at[0])
-    own_e.start()
-    own_i = pltpu.make_async_copy(ids_ref, ids_z.at[0], zi_recv)
-    own_i.start()
-    for k in order[1:]:
-        to = (lax.rem(z + k, nz) * NX + x, trk)
-        pltpu.make_async_remote_copy(
-            src_ref=ids_ref, dst_ref=ids_z.at[order.index(nz - k)], send_sem=zi_send, recv_sem=zi_recv,
-            device_id=to, device_id_type=MESH).start()
-    for k in order[1:]:
-        to = (lax.rem(z + k, nz) * NX + x, trk)
-        i = order.index(nz - k)
-        pltpu.make_async_remote_copy(
-            src_ref=embed_ref, dst_ref=emb_z.at[i], send_sem=z_send, recv_sem=z_recv.at[i],
-            device_id=to, device_id_type=MESH).start()
-
-    before = (z * NX + x, lax.rem(trk + nt - 1, nt))
-    k_copy = pltpu.make_async_remote_copy(
-        src_ref=key_ref, dst_ref=kn_ref, send_sem=kv_send.at[0], recv_sem=kv_recv.at[0],
-        device_id=before, device_id_type=MESH)
-    v_copy = pltpu.make_async_remote_copy(
-        src_ref=value_ref, dst_ref=vn_ref, send_sem=kv_send.at[1], recv_sem=kv_recv.at[1],
-        device_id=before, device_id_type=MESH)
-    k_copy.start()
-    v_copy.start()
-
-    await_bytes(ids_z, zi_recv)
-    lane = iota((listing, cols), 1) // rows
-    ids = ids_z[0, :listing, :]
-    most = ids_z[0, listing:, :128]
-    for i in range(1, nz):
-        ids = jnp.where(lane == i, ids_z[i, :listing, :], ids)
-        most = jnp.maximum(most, ids_z[i, listing:, :128])
-    most_one[...] = most
-    pltpu.make_async_copy(most_one, most_all.at[me], most_rsem).start()
-    in_plane(lambda p, to: pltpu.make_async_remote_copy(
-        src_ref=most_one, dst_ref=most_all.at[me], send_sem=most_ssem, recv_sem=most_rsem,
-        device_id=to, device_id_type=MESH).start())
-
-    view = z * npl + iota((npl, cols), 0)
-    named = jnp.zeros((npl, cols), F32)
-    for j in range(listing):
-        named = jnp.where(ids[j : j + 1, :] == view, 1.0, named)
-    named_b = named.astype(BF)
-    c0 = iota((cols, cols), 0)
-    c1 = iota((cols, cols), 1)
-    earlier = jnp.where((c0 < c1) & (c0 // rows == c1 // rows), 1.0, 0.0).astype(BF)
-    rank = jnp.dot(named_b, earlier, preferred_element_type=F32)
-    ranked = jnp.where(named > 0.5, rank, -1.0)
-
-    same_z = iota((per, gcols), 0) // CAP == iota((per, gcols), 1) // rows
-    slot_r = (iota((per, gcols), 0) % CAP).astype(F32)
-    v0 = iota((npl, npl), 0)
-    v1 = iota((npl, npl), 1)
-    before_v = jnp.where(v0 < v1, 1.0, 0.0).astype(BF)
-    t0 = iota((per, npl), 0)
-    tr = (t0 % CAP).astype(F32)
-    for g in range(2):
-        counts = nt_dot(jnp.where(same_z, 1.0, 0.0).astype(BF), named_b[:, g * gcols : (g + 1) * gcols])
-        base = jnp.dot(counts.astype(BF), before_v, preferred_element_type=F32)
-        target_ref[g] = jnp.where(tr < counts, base + tr, -1.0)
-
-    for g in range(2):
-        for i in range(g * half, (g + 1) * half):
-            await_bytes(emb_z.at[i], z_recv.at[i])
-        states = emb_z[g * half : (g + 1) * half].reshape(gcols, width).astype(F32)
-        states = layer_norm(states) * gain_ref[...]
-        high = states.astype(BF)
-        rest = states - high.astype(F32)
-        middle = rest.astype(BF)
-        low = (rest - middle.astype(F32)).astype(BF)
-        parts = jnp.concatenate([high, middle, low], axis=0)
-        picks = []
-        for v in range(npl):
-            here = ranked[v : v + 1, g * gcols : (g + 1) * gcols]
-            picks.append(jnp.where(same_z & (here == slot_r), 1.0, 0.0).astype(BF))
-        pick = jnp.concatenate(picks, axis=0)
-        pick = jnp.concatenate([pick, pick, pick], axis=1)
-        made = jnp.dot(pick, parts, preferred_element_type=F32)
-        frow = grows // NX
-        for f in range(NX):
-            at = slice(f * frow, (f + 1) * frow)
-            q_send[g, at] = (made[at] + code_ref[f : f + 1, :]).astype(BF)
-        pltpu.make_async_copy(q_send.at[g, mine], q_recv.at[g, mine], q_rsem.at[g]).start()
-        in_plane(lambda p, to: pltpu.make_async_remote_copy(
-            src_ref=q_send.at[g, part(p)], dst_ref=q_recv.at[g, mine],
-            send_sem=q_ssem.at[g], recv_sem=q_rsem.at[g], device_id=to, device_id_type=MESH).start())
-
-    def attend(g, c):
-        @pl.loop(0, grows // block)
-        def _(b):
-            at = pl.ds(pl.multiple_of(b * block, block), block)
-            for h in range(wide // head):
-                lanes = slice(c * wide + h * head, c * wide + (h + 1) * head)
-                q = q_recv[g, at, lanes]
-                s0 = nt_dot(q, key_ref[:, lanes])
-                s1 = nt_dot(q, kn_ref[:, lanes])
-                top = jnp.maximum(jnp.max(s0, axis=-1, keepdims=True), jnp.max(s1, axis=-1, keepdims=True))
-                w0 = jnp.exp2((s0 - top) * scale)
-                w1 = jnp.exp2((s1 - top) * scale)
-                sums = jnp.sum(w0, axis=-1, keepdims=True) + jnp.sum(w1, axis=-1, keepdims=True)
-                o = jnp.dot(w0.astype(BF), value_ref[:, lanes], preferred_element_type=F32)
-                o = o + jnp.dot(w1.astype(BF), vn_ref[:, lanes], preferred_element_type=F32)
-                a_send[g * chunks + c, at, h * head : (h + 1) * head] = (o / sums).astype(BF)
-
-    def send_in_plane(n):
-        pltpu.make_async_copy(a_send.at[n, mine], a_recv.at[n, mine], a_rsem.at[n]).start()
-        in_plane(lambda p, to: pltpu.make_async_remote_copy(
-            src_ref=a_send.at[n, part(p)], dst_ref=a_recv.at[n, mine],
-            send_sem=a_ssem.at[n], recv_sem=a_rsem.at[n], device_id=to, device_id_type=MESH).start())
+            px, pt = lax.div(p, nt), lax.rem(p, nt)
+            dy = lax.rem(lax.div(pt, CORES) + ny - y, ny)
+            pltpu.make_async_remote_copy(
+                src_ref=a_send.at[n, rows_of(px * CORES + lax.rem(pt, CORES), dy)], dst_ref=a_recv.at[n, mine],
+                send_sem=a_ssem.at[n], recv_sem=a_rsem.at[n],
+                device_id=(z * NX + px, pt), device_id_type=MESH).start()
 
     def send_along_z(n):
         g, c = n // chunks, n % chunks
@@ -243,8 +317,8 @@
                     src_ref=src, dst_ref=back_ref.at[c, line], send_sem=b_ssem.at[n], recv_sem=b_rsem.at[n],
                     device_id=(lax.rem(z + dz, nz) * NX + x, trk), device_id_type=MESH).start()
 
-    k_copy.wait()
-    v_copy.wait()
+    for copy in copies:
+        copy.wait()
     for n in range(2 * chunks):
         g, c = n // chunks, n % chunks
         if c == 0:
@@ -263,13 +337,15 @@
             send_along_z(n - 1)
     send_along_z(2 * chunks - 1)
 
+    await_bytes(ids_y.at[pl.ds(0, ny - 1)], yi_send)
+    await_bytes(emb_z.at[0, pl.ds(0, ny - 1)], y_send)
     await_bytes(emb_z.at[pl.ds(0, nz - 1)], z_send)
     await_bytes(ids_z.at[pl.ds(0, nz - 1)], zi_send)
-    await_bytes(most_all.at[pl.ds(0, npl - 1)], most_ssem)
+    await_bytes(most_all.at[pl.ds(0, nx - 1)], most_ssem)
     await_bytes(most_all, most_rsem)
     most_ref[...] = jnp.max(most_all[...], axis=0)
     for g in range(2):
-        await_bytes(q_send.at[g, pl.ds(0, (npl - 1) * per)], q_ssem.at[g])
+        await_bytes(q_send.at[g, pl.ds(0, (nx - 1) * lot)], q_ssem.at[g])
     for n in range(2 * chunks):
         remote = sum(1 for i in range(half) if order[n // chunks * half + i] != 0)
         await_bytes(a_send.at[n, pl.ds(0, (npl - 1) * per)], a_ssem.at[n])
@@ -375,6 +451,7 @@
     tm_count = lax.axis_size("tm")
     nt = lax.axis_size("trk")
     nz = tm_count // NX
+    ny = nt // CORES
     npl = NX * nt
     rows, width = track_embed.shape
     listing = view_ids.shape[1]
@@ -399,7 +476,7 @@
     in_plane_of = jnp.arange(nz, dtype=jnp.int32)
     crowd = jnp.max(jnp.sum((plane[None, :] == in_plane_of[:, None]).astype(jnp.int32), axis=1))
     turned = jnp.concatenate(
-        [jnp.tile(shown.T, (1, nz)), jnp.broadcast_to(crowd, (8, nz * rows))], axis=0)
+        [jnp.tile(shown.T, (1, ny)), jnp.broadcast_to(crowd, (8, ny * rows))], axis=0)
 
     anywhere = pl.BlockSpec(memory_space=pl.ANY)
     vmem = pl.BlockSpec(memory_space=pltpu.VMEM)
@@ -417,25 +494,26 @@
             jax.ShapeDtypeStruct((chunks, nz * cap, wide), BF),
             jax.ShapeDtypeStruct((count, grows, wide), BF),
             jax.ShapeDtypeStruct((2, per, npl), F32),
-            jax.ShapeDtypeStruct((8, 128), jnp.int32),
+            jax.ShapeDtypeStruct((8, ny * rows), jnp.int32),
         ),
-        in_specs=[vmem] * 6,
+        in_specs=[vmem] * 4 + [anywhere] * 2,
         out_specs=(anywhere, anywhere, vmem, vmem),
         scratch_shapes=[
-            pltpu.VMEM((nz, rows, width), BF),
-            pltpu.VMEM((nz, listing + 8, nz * rows), jnp.int32),
+            pltpu.VMEM((nz, ny, rows, width), BF),
+            pltpu.VMEM((ny, listing + 8, ny * rows), jnp.int32),
+            pltpu.VMEM((nz, listing + 8, ny * rows), jnp.int32),
             pltpu.VMEM((2, grows, width), BF),
             pltpu.VMEM((2, grows, width), BF),
-            pltpu.VMEM((tokens, width), BF),
-            pltpu.VMEM((tokens, width), BF),
+            pltpu.VMEM((2 * tokens, width), BF),
+            pltpu.VMEM((2 * tokens, width), BF),
             pltpu.VMEM((count, grows, wide), BF),
             pltpu.VMEM((count, grows, wide), BF),
             pltpu.VMEM((2, grows, nz // 2 * cap), BF),
             pltpu.VMEM((count, nz // 2 * cap, wide), BF),
-            pltpu.VMEM((8, 128), jnp.int32),
-            pltpu.VMEM((npl, 8, 128), jnp.int32),
-            dma, dma((nz,)), dma, dma, dma((2,)), dma((2,)), dma((2,)), dma((2,)),
-            dma((count,)), dma((count,)), dma((count,)), dma((count,)), dma, dma, dma((count,)),
+            pltpu.VMEM((8, ny * rows), jnp.int32),
+            pltpu.VMEM((NX * CORES, 8, ny * rows), jnp.int32),
+            dma, dma, dma, dma, dma, dma((nz,)), dma, dma((nz,)), dma((2,)), dma((2,)), dma((2,)),
+            dma((2,)), dma((2,)), dma((count,)), dma((count,)), dma((count,)), dma((count,)), dma, dma, dma((count,)),
         ],
         compiler_params=pltpu.CompilerParams(
             collective_id=0, has_side_effects=True, vmem_limit_bytes=52 * 1024 * 1024),

time: 143 us -> 134 us (0.937)
  Pallas kernels: 130 us -> 122 us
    pallas_call x1, Pallas kernels: 110 us -> 101 us  [local(): pl.pallas_call(functools.partial(mega_kernel, nz, nt, rows, cap, chunks,...]
where the time goes in v3:
time: 134 us; the launch traced here: 133 us
  Pallas kernels  122 us (91%)
  local copies, waits for them, and re-layouts  6.4 us (5%)
  other arithmetic  2.68 us (2%)
  between operations  1.48 us (1%)
    pallas_call x1, Pallas kernels, local(): pl.pallas_call(functools.partial(mega_kernel, nz, nt, rows, cap, chunks,...  101 us
    pallas_call x1, Pallas kernels, finish(): pl.pallas_call(functools.partial(track_kernel, chunks, len(backs), cap),...  20.9 us

profile of v3, /device:TPU:33, one launch (start us, length us, event | category | flops | bytes accessed | tf_op | source)
XLA Modules:
  0.0 132.6 jit_solution(11171072921151200797)
XLA Ops:
  0.6 0.0 copy-start.4
  0.7 0.0 copy-start.6
  0.7 0.7 fusion
  1.4 0.1 copy.33
  1.5 0.1 lt.52
  1.6 0.1 copy.35
  1.7 0.1 reshape.244
  1.8 0.1 multiply_sine_fusion
  1.9 0.7 iota_add_fusion
  2.6 0.1 copy.32
  2.7 0.1 reshape.237
  2.8 0.1 reshape.240
  2.9 0.3 convert_reduce_fusion
  3.3 0.1 convert_reduce_fusion.1
  3.4 0.6 reduce_max.9
  4.0 0.1 tile.10
  4.1 0.6 concatenate.6.ids_ref
  4.8 0.0 copy-start.1
  4.8 1.2 copy-done.1
  6.0 101.0 %mega.1 = (bf16[2,512,512]{2,1,0:T(8,128)(2,1)}, bf16[4,512,512]{2,1,0:T(8,128)(2,1)}, f32[2,16,32]{2,1,0:T(8,128)S(1)}, s32[8,128]{1,0:T(8,128)S(1)}) custom-call(bf16[32,1024]{1,0:T(8,128)(2,1)} %embed_ref.1, s32[24,128]{1,0:T(8,128)S(1)} %concatenate.6.ids_ref, f32[4,1024]{1,0:T(4,128)S(1)} %pad_maximum_fusion.code_ref, f32[1,1024]{1,0:T(1,128)} %bitcast.15, ...), custom_call_target="tpu_custom_call" | custom-call | tf_op jit(solution)/shard_map/mega/pallas_call | solution.py:491
  107.0 0.5 slice.3
  108.1 0.0 copy-done.4
  108.1 0.0 copy-done.5
  108.1 0.0 copy-done.8
  108.2 0.0 copy-done.7
  108.2 0.0 copy-done.9
  108.2 23.6 %conditional.1 = ((bf16[512,1024]{1,0:T(8,128)(2,1)}, f32[512,10]{1,0:T(8,128)S(1)})) conditional(s32[]{:T(128)} %bitcast.4, (bf16[2,512,512]{2,1,0:T(8,128)(2,1)}, s32[512,1]{0,1:T(1,128)S(1)}, bf16[32,1024]{1,0:T(8,128)(2,1)S(1)}, f32[1,1024]{1,0:T(1,128)S(1)}, f32[512,1]{0,1:T(1,128)S(1)}, /*index=5*/f32[1,512]{1,0:T(1,128)S(1)}, ...), branch_computations={%region_3.4_spmd, %region_4.5_spmd} | conditional | bytes 8417344 | solution.py:562
  108.4 0.8 copy.38.refs_12_
  109.2 0.9 copy.37.refs_4_
  110.0 0.9 copy.36.refs_1_
  110.9 20.9 %track.2 = (bf16[512,1024]{1,0:T(8,128)(2,1)}, f32[512,10]{1,0:T(8,128)S(1)}) custom-call(bf16[2,512,512]{2,1,0:T(8,128)(2,1)} %get-tuple-element.62.refs_0_, s32[512,1]{1,0:T(8,128)} %copy.36.refs_1_, bf16[32,1024]{1,0:T(8,128)(2,1)S(1)} %get-tuple-element.64.refs_2_, f32[1,1024]{1,0:T(1,128)S(1)} %get-tuple-element.65.refs_3_, f32[512,1]{1,0:T(8,128)} %copy.37.refs_4_, ...), custom_call_target="tpu_custom_call" | custom-call | tf_op jit(solution)/shard_map/cond/branch_0_fun/track/pallas_call | solution.py:531
  131.8 0.8 copy.43
  (14 shorter events, 0.1 us)
Async XLA Ops:
  0.6 107.5 %copy-start.4 = (bf16[32,1024]{1,0:T(8,128)(2,1)S(1)}, bf16[32,1024]{1,0:T(8,128)(2,1)}, u32[]{:S(2)}) copy-start(bf16[32,1024]{1,0:T(8,128)(2,1)} %embed_ref.1) | copy-start | bytes 196612
  0.6 107.5 %copy-start.5 = (bf16[512,10]{0,1:T(8,128)(2,1)S(1)}, bf16[512,10]{0,1:T(8,128)(2,1)}, u32[]{:S(2)}) copy-start(bf16[512,10]{0,1:T(8,128)(2,1)} %param.27) | copy-start | bytes 30724
  0.7 107.5 %copy-start.8 = (f32[512]{0:T(512)S(1)}, f32[512]{0:T(512)}, u32[]{:S(2)}) copy-start(f32[512]{0:T(512)} %param.26) | copy-start | bytes 6148
  0.7 107.5 %copy-start.7 = (f32[1024]{0:T(1024)S(1)}, f32[1024]{0:T(1024)}, u32[]{:S(2)}) copy-start(f32[1024]{0:T(1024)} %param.24) | copy-start | bytes 12292
  0.7 107.5 %copy-start.9 = (f32[8]{0:T(128)S(1)}, f32[8]{0:T(128)}, u32[]{:S(2)}) copy-start(f32[8]{0:T(128)} %param.22) | copy-start | bytes 100
  0.7 107.5 %copy-start.6 = (f32[1024]{0:T(1024)S(1)}, f32[1024]{0:T(1024)}, u32[]{:S(2)}) copy-start(f32[1024]{0:T(1024)} %param.20) | copy-start | bytes 12292
  4.8 1.2 copy-start.1
  6.0 102.2 %copy-start.2 = (bf16[1024,1024]{1,0:T(8,128)(2,1)S(1)}, bf16[1024,1024]{1,0:T(8,128)(2,1)}, u32[]{:S(2)}) copy-start(bf16[1024,1024]{1,0:T(8,128)(2,1)} %param.23) | copy-start | bytes 6291460

commit v4 on v3

--- a/solution.py
+++ b/solution.py
@@ -78,17 +78,16 @@
 
 
 def z_order(nz):
-    near = [0]
-    for k in range(1, nz // 2 + 1):
-        near += [k] if 2 * k == nz else [k, nz - k]
-    return near
+    half = nz // 2
+    middle = [k for d in range(2, half) for k in (d, nz - d)]
+    return middle + [0, 1, nz - 1, half]
 
 
 def mega_kernel(
     nz, nt, rows, cap, chunks, block,
     embed_ref, ids_ref, code_ref, gain_ref, key_ref, value_ref,
     back_ref, kept_ref, target_ref, most_ref,
-    emb_z, ids_y, ids_z, q_send, q_recv, kk_ref, vv_ref, a_send, a_recv, moves, b_send, most_one, most_all,
+    emb_z, ids_y, ids_z, parts, q_send, q_recv, kk_ref, vv_ref, a_send, a_recv, moves, b_send, most_one, most_all,
     y_send, y_recv, yi_send, yi_recv, z_send, z_recv, zi_send, zi_recv, kv_own, kv_send, kv_recv,
     q_ssem, q_rsem, a_ssem, a_rsem, b_ssem, b_rsem, most_ssem, most_rsem, keep_sem,
 ):
@@ -149,27 +148,26 @@
     ids_z[0, listing:, :] = most
     await_bytes(emb_z.at[0], y_recv)
 
-    def to_z(source, step, part=None):
+    def to_z(source, step, part):
         target = (source - step) % nz
         device = (lax.rem(z + nz + step, nz) * NX + x, trk)
-        if part is None or part == 0:
+        if part == 0:
             pltpu.make_async_remote_copy(
                 src_ref=ids_z.at[source], dst_ref=ids_z.at[target], send_sem=zi_send, recv_sem=zi_recv.at[target],
                 device_id=device, device_id_type=MESH).start()
-        src, dst = emb_z.at[source], emb_z.at[target]
-        if part is not None:
-            few = pl.ds(part * (ny // 2), ny // 2)
-            src, dst = emb_z.at[source, few], emb_z.at[target, few]
+        few = pl.ds(part * (ny // 2), ny // 2)
         pltpu.make_async_remote_copy(
-            src_ref=src, dst_ref=dst, send_sem=z_send, recv_sem=z_recv.at[target],
-            device_id=device, device_id_type=MESH).start()
-
-    def arrive(slot):
-        await_bytes(ids_z.at[slot], zi_recv.at[slot])
-        await_bytes(emb_z.at[slot], z_recv.at[slot])
-
-    to_z(0, 1)
-    to_z(0, -1)
+            src_ref=emb_z.at[source, few], dst_ref=emb_z.at[target, few], send_sem=z_send,
+            recv_sem=z_recv.at[2 * target + part], device_id=device, device_id_type=MESH).start()
+
+    def arrive(slot, part):
+        if part == 0:
+            await_bytes(ids_z.at[slot], zi_recv.at[slot])
+        await_bytes(emb_z.at[slot, pl.ds(part * (ny // 2), ny // 2)], z_recv.at[2 * slot + part])
+
+    for part in range(2):
+        to_z(0, 1, part)
+        to_z(0, -1, part)
     for copy in copies:
         copy.start()
 
@@ -195,36 +193,41 @@
             named = jnp.where(ids[j : j + 1, :] == view, 1.0, named)
         return named
 
+    ranked, found = {}, {}
+
+    def prepare(slot):
+        ids = ids_z[slot, :listing, :]
+        named = names(ids, view_x)
+        rank = jnp.dot(named.astype(BF), earlier, preferred_element_type=F32)
+        ranked[slot] = jnp.where(named > 0.5, rank, -1.0)
+        here = jnp.where((slot_row // CAP == order.index(slot) % half) & own_lane, 1.0, 0.0).astype(BF)
+        found[slot] = nt_dot(here, names(ids, view_p).astype(BF))
+        states = layer_norm(emb_z[slot].reshape(lanes, width).astype(F32)) * gain_ref[...]
+        high = states.astype(BF)
+        rest = states - high.astype(F32)
+        middle = rest.astype(BF)
+        parts[0, slot] = high
+        parts[1, slot] = middle
+        parts[2, slot] = (rest - middle.astype(F32)).astype(BF)
+
     def build(g):
         slots = order[g * half : (g + 1) * half]
-        ranked, parts = [], []
-        counts = jnp.zeros((per, npl), F32)
-        for i, slot in enumerate(slots):
-            ids = ids_z[slot, :listing, :]
-            named = names(ids, view_x)
-            rank = jnp.dot(named.astype(BF), earlier, preferred_element_type=F32)
-            ranked.append(jnp.where(named > 0.5, rank, -1.0))
-            here = jnp.where((slot_row // CAP == i) & own_lane, 1.0, 0.0).astype(BF)
-            counts = counts + nt_dot(here, names(ids, view_p).astype(BF))
-            states = layer_norm(emb_z[slot].reshape(lanes, width).astype(F32)) * gain_ref[...]
-            high = states.astype(BF)
-            rest = states - high.astype(F32)
-            middle = rest.astype(BF)
-            low = (rest - middle.astype(F32)).astype(BF)
-            parts.append((high, middle, low))
+        counts = found[slots[0]]
+        for slot in slots[1:]:
+            counts = counts + found[slot]
         base = jnp.dot(counts.astype(BF), before_v, preferred_element_type=F32)
         target_ref[g] = jnp.where(tr < counts, base + tr, -1.0)
         for dy in range(ny):
             here = jnp.zeros((nx, lanes), F32)
             for i in range(half):
                 shift = (i - dy) * rows % lanes
-                moved = pltpu.roll(ranked[i], shift, 1) if shift else ranked[i]
+                moved = pltpu.roll(ranked[slots[i]], shift, 1) if shift else ranked[slots[i]]
                 here = jnp.where(lane_at == i, moved, here)
             picks = [jnp.where(same_z & (here[v : v + 1, :] == slot_r), 1.0, 0.0).astype(BF) for v in range(nx)]
             pick = jnp.concatenate(picks, axis=0)
             pick = jnp.concatenate([pick, pick, pick], axis=1)
             at = slice(dy * rows, (dy + 1) * rows)
-            source = jnp.concatenate([parts[i][k][at] for k in range(3) for i in range(half)], axis=0)
+            source = jnp.concatenate([parts[k, slots[i], at] for k in range(3) for i in range(half)], axis=0)
             made = jnp.dot(pick, source, preferred_element_type=F32)
             for v in range(nx):
                 f = v // CORES
@@ -239,20 +242,21 @@
                 send_sem=q_ssem.at[g], recv_sem=q_rsem.at[g],
                 device_id=(z * NX + lax.div(p, CORES), y * CORES + lax.rem(p, CORES)), device_id_type=MESH).start()
 
+    prepare(0)
     for k in range(1, half):
-        arrive(nz - k)
-        if k < half - 1:
-            to_z(nz - k, 1)
-        else:
-            to_z(nz - k, 1, 0)
-        arrive(k)
-        if k < half - 1:
-            to_z(k, -1)
-        else:
-            to_z(k, -1, 1)
-        if k == 2:
-            build(0)
-    arrive(half)
+        for part in range(2):
+            arrive(nz - k, part)
+            if k < half - 1 or part == 0:
+                to_z(nz - k, 1, part)
+            arrive(k, part)
+            if k < half - 1 or part == 1:
+                to_z(k, -1, part)
+        prepare(nz - k)
+        prepare(k)
+    build(0)
+    for part in range(2):
+        arrive(half, part)
+    prepare(half)
     build(1)
 
     most = ids_z[0, listing:, :]
@@ -400,11 +404,17 @@
 ):
     backs, refs = refs[:lists], refs[lists:]
     (
-        slot_ref, embed_ref, gain_ref, valid_ref, keys_ref, scale_ref,
-        wt_ref, wm_ref, bgain_ref, wh_ref, bh_ref, wb_ref,
+        slot_ref, embed_ref, gain_ref, count_ref, scale_ref, bgain_ref, bh_ref, wb_ref,
+        wt_any, wm_any, wh_any,
         refined_ref, box_ref,
-        projected, mixed,
+        projected, mixed, wt_ref, wm_ref, wh_ref, load_sem,
     ) = refs
+    loads = [
+        pltpu.make_async_copy(far, near, load_sem.at[i])
+        for i, (far, near) in enumerate(((wt_any, wt_ref), (wm_any, wm_ref), (wh_any, wh_ref)))
+    ]
+    for load in loads:
+        load.start()
     rows, width = embed_ref.shape
     entries = slot_ref.shape[0]
     listing = entries // rows
@@ -420,28 +430,39 @@
     states = jnp.broadcast_to(states[:, None, :], (rows, listing, width)).reshape(entries, width)
     residual = states + attended
     normed = layer_norm(residual).astype(BF)
+    loads[0].wait()
     projected[...] = jnp.dot(normed, wt_ref[...], preferred_element_type=F32).astype(BF)
     block = 128
     head = width // HEADS
-    same = iota((block, block), 0) // listing == iota((block, block), 1) // listing
+    row = iota((block, block), 0) // listing
+    col = iota((block, block), 1)
     for b in range(entries // block):
         at = slice(b * block, (b + 1) * block)
-        open_keys = same & (keys_ref[:, at] > 0.5)
+        open_keys = (row == col // listing) & (col % listing < count_ref[0:1, at])
+        scores = []
         for h in range(HEADS):
             q = projected[at, h * head : (h + 1) * head]
             k = projected[at, width + h * head : width + (h + 1) * head]
+            scores.append(nt_dot(q, k) * (scale_ref[0, h] * head ** (-0.5)))
+        scores = jnp.where(open_keys[None], jnp.stack(scores, axis=0), MASKED)
+        weights = jnp.exp(scores - jnp.max(scores, axis=-1, keepdims=True))
+        probs = (weights * (1.0 / jnp.sum(weights, axis=-1, keepdims=True))).astype(BF)
+        for h in range(HEADS):
             v = projected[at, 2 * width + h * head : 2 * width + (h + 1) * head]
-            scores = nt_dot(q, k) * (scale_ref[0, h] * head ** (-0.5))
-            scores = jnp.where(open_keys, scores, MASKED)
-            weights = jnp.exp(scores - jnp.max(scores, axis=-1, keepdims=True))
-            probs = (weights / jnp.sum(weights, axis=-1, keepdims=True)).astype(BF)
-            mixed[at, h * head : (h + 1) * head] = jnp.dot(probs, v, preferred_element_type=F32).astype(BF)
+            mixed[at, h * head : (h + 1) * head] = jnp.dot(probs[h], v, preferred_element_type=F32).astype(BF)
+    loads[1].wait()
     updated = residual + jnp.dot(mixed[...], wm_ref[...], preferred_element_type=F32)
-    valid = valid_ref[...]
-    refined_ref[...] = (updated * valid).astype(BF)
+    refined_ref[...] = jnp.where(slot_ref[...] >= 0, updated, 0.0).astype(BF)
     box_input = (layer_norm(updated) * bgain_ref[...]).astype(BF)
+    loads[2].wait()
     hidden = jax.nn.gelu(jnp.dot(box_input, wh_ref[...], preferred_element_type=F32) + bh_ref[...]).astype(BF)
-    box_ref[...] = jnp.dot(hidden, wb_ref[...], preferred_element_type=F32) * valid
+    i0 = iota((entries, entries), 0)
+    turn = jnp.where(iota((entries, entries), 1) == i0 % rows * listing + i0 // rows, 1.0, 0.0).astype(BF)
+    hidden = jnp.dot(turn, hidden, preferred_element_type=F32).astype(BF)
+    boxes = nt_dot(wb_ref[...], hidden)
+    boxes = jnp.where(iota(boxes.shape, 1) // rows < count_ref[1:2, :], boxes, 0.0)
+    for j in range(listing):
+        box_ref[:, j, :] = boxes[:, j * rows : (j + 1) * rows]
 
 
 def local(
@@ -502,6 +523,7 @@
             pltpu.VMEM((nz, ny, rows, width), BF),
             pltpu.VMEM((ny, listing + 8, ny * rows), jnp.int32),
             pltpu.VMEM((nz, listing + 8, ny * rows), jnp.int32),
+            pltpu.VMEM((3, nz, ny * rows, width), BF),
             pltpu.VMEM((2, grows, width), BF),
             pltpu.VMEM((2, grows, width), BF),
             pltpu.VMEM((2 * tokens, width), BF),
@@ -512,7 +534,7 @@
             pltpu.VMEM((count, nz // 2 * cap, wide), BF),
             pltpu.VMEM((8, ny * rows), jnp.int32),
             pltpu.VMEM((NX * CORES, 8, ny * rows), jnp.int32),
-            dma, dma, dma, dma, dma, dma((nz,)), dma, dma((nz,)), dma((2,)), dma((2,)), dma((2,)),
+            dma, dma, dma, dma, dma, dma((2 * nz,)), dma, dma((nz,)), dma((2,)), dma((2,)), dma((2,)),
             dma((2,)), dma((2,)), dma((count,)), dma((count,)), dma((count,)), dma((count,)), dma, dma, dma((count,)),
         ],
         compiler_params=pltpu.CompilerParams(
@@ -520,11 +542,11 @@
         name="mega",
     )(track_embed, turned, codes, gain, keys, values)
 
-    seen = valid.astype(F32)
     boxes_wide = w_box.shape[1]
+    counts = jnp.stack([jnp.repeat(view_count, listing), jnp.tile(view_count, listing)])
     shared = (
-        slot, track_embed, gain, seen.reshape(entries, 1), seen.reshape(1, entries), temporal_scale[None, :],
-        w_temporal, w_merge, box_gain[None, :], w_hidden, b_hidden[None, :], w_box,
+        slot, track_embed, gain, counts, temporal_scale[None, :], box_gain[None, :], b_hidden[None, :], w_box.T,
+        w_temporal, w_merge, w_hidden,
     )
 
     def finish(*backs):
@@ -532,11 +554,18 @@
             functools.partial(track_kernel, chunks, len(backs), cap),
             out_shape=(
                 jax.ShapeDtypeStruct((entries, width), BF),
-                jax.ShapeDtypeStruct((entries, boxes_wide), F32),
+                jax.ShapeDtypeStruct((boxes_wide, listing, rows), F32),
             ),
-            in_specs=[vmem] * (len(backs) + 5) + [pl.BlockSpec(memory_space=pltpu.SMEM)] + [vmem] * 6,
+            in_specs=[vmem] * (len(backs) + 4) + [pl.BlockSpec(memory_space=pltpu.SMEM)] + [vmem] * 3 + [anywhere] * 3,
             out_specs=(vmem, vmem),
-            scratch_shapes=[pltpu.VMEM((entries, 3 * width), BF), pltpu.VMEM((entries, width), BF)],
+            scratch_shapes=[
+                pltpu.VMEM((entries, 3 * width), BF),
+                pltpu.VMEM((entries, width), BF),
+                pltpu.VMEM(w_temporal.shape, BF),
+                pltpu.VMEM(w_merge.shape, BF),
+                pltpu.VMEM(w_hidden.shape, BF),
+                dma((3,)),
+            ],
             compiler_params=pltpu.CompilerParams(vmem_limit_bytes=56 * 1024 * 1024),
             name="track",
         )(*backs, *shared)
@@ -560,7 +589,7 @@
         return finish(back, rest)
 
     refined, boxes = lax.cond(most[0, 0] > cap, finish_long, lambda: finish(back))
-    return refined.reshape(rows, listing, width), boxes.reshape(rows, listing, boxes_wide)
+    return refined.reshape(rows, listing, width), jnp.transpose(boxes, (2, 1, 0))
 
 
 def solution(mesh):

time: 134 us -> 121 us (0.903); the launches traced: 133 us -> 121 us
  Pallas kernels: 122 us -> 111 us
    pallas_call x1, Pallas kernels: 20.9 us -> 13.8 us  [finish(): pl.pallas_call(functools.partial(track_kernel, chunks, len(backs), cap),...]
    pallas_call x1, Pallas kernels: 101 us -> 97.5 us  [local(): pl.pallas_call(functools.partial(mega_kernel, nz, nt, rows, cap, chunks,...]
where the time goes in v4:
time: 121 us
  Pallas kernels  111 us (92%)
  local copies, waits for them, and re-layouts  5.33 us (4%)
  other arithmetic  2.69 us (2%)
  between operations  1.65 us (1%)
    pallas_call x1, Pallas kernels, local(): pl.pallas_call(functools.partial(mega_kernel, nz, nt, rows, cap, chunks,...  97.5 us
    pallas_call x1, Pallas kernels, finish(): pl.pallas_call(functools.partial(track_kernel, chunks, len(backs), cap),...  13.8 us

profile of v4, /device:TPU:33, one launch (start us, length us, event | category | flops | bytes accessed | tf_op | source)
XLA Modules:
  0.0 121.2 jit_solution(2618778624815720024)
XLA Ops:
  0.6 0.0 copy-start.4
  0.6 0.0 copy-start.5
  0.7 0.0 copy-start.8
  0.7 0.0 copy-start.7
  0.7 0.0 copy-start.9
  0.7 0.0 copy-start.6
  0.7 0.7 iota_compare_fusion.1
  1.4 0.1 copy.25
  1.5 0.1 lt.40
  1.6 0.7 tile.8
  2.3 0.1 stack_tile.3
  2.3 0.1 multiply_sine_fusion
  2.5 0.7 lt.38.clone
  3.2 0.1 stack_reshape.3
  3.3 0.7 iota_add_fusion
  4.0 0.1 copy.24
  4.1 0.1 reshape.187
  4.2 0.1 reshape.190
  4.3 0.3 convert_reduce_fusion
  4.7 0.1 convert_reduce_fusion.1
  4.8 0.6 reduce_max.9
  5.4 0.1 tile.7
  5.5 0.6 concatenate.6.ids_ref
  6.2 0.0 copy-start.1
  6.2 1.2 %copy-done.1 = bf16[1,1,512,1024]{3,2,1,0:T(8,128)(2,1)S(1)} copy-done((bf16[1,1,512,1024]{3,2,1,0:T(8,128)(2,1)S(1)}, bf16[1,1,512,1024]{3,2,1,0:T(8,128)(2,1)}, u32[]{:S(2)}) %copy-start.1) | copy-done | bytes 1048600
  7.4 97.5 %mega.1 = (bf16[2,512,512]{2,1,0:T(8,128)(2,1)}, bf16[4,512,512]{2,1,0:T(8,128)(2,1)}, f32[2,16,32]{2,1,0:T(8,128)S(1)}, s32[8,128]{1,0:T(8,128)S(1)}) custom-call(bf16[32,1024]{1,0:T(8,128)(2,1)} %embed_ref.1, s32[24,128]{1,0:T(8,128)S(1)} %concatenate.6.ids_ref, f32[4,1024]{1,0:T(4,128)S(1)} %pad_maximum_fusion.code_ref, f32[1,1024]{1,0:T(1,128)} %bitcast.18, ...), custom_call_target="tpu_custom_call" | custom-call | tf_op jit(solution)/shard_map/mega/pallas_call | solution.py:512
  104.9 0.5 slice.3
  106.1 0.0 copy-done.4
  106.1 0.0 copy-done.5
  106.1 14.9 %conditional.1 = (f32[10,16,32]{2,1,0:T(8,128)}, bf16[32,16,1024]{2,1,0:T(8,128)(2,1)}) conditional(s32[]{:T(128)} %bitcast.6, (bf16[2,512,512]{2,1,0:T(8,128)(2,1)}, s32[512,1]{0,1:T(1,128)S(1)}, bf16[32,1024]{1,0:T(8,128)(2,1)S(1)}, f32[1,1024]{1,0:T(1,128)S(1)}, s32[2,512]{1,0:T(2,128)S(1)}, /*index=5*/f32[1,8]{1,0:T(1,128)S(1)}, ...), branch_computations={%region_3.4_spmd, %region_4.5_spmd} | conditional | bytes 8392776 | solution.py:591
  106.2 0.9 copy.28.refs_1_
  107.0 13.8 %track.2 = (bf16[512,1024]{1,0:T(8,128)(2,1)}, f32[10,16,32]{2,1,0:T(8,128)}) custom-call(bf16[2,512,512]{2,1,0:T(8,128)(2,1)} %get-tuple-element.57.refs_0_, s32[512,1]{1,0:T(8,128)} %copy.28.refs_1_, bf16[32,1024]{1,0:T(8,128)(2,1)S(1)} %get-tuple-element.59.refs_2_, f32[1,1024]{1,0:T(1,128)S(1)} %get-tuple-element.60.refs_3_, ...), custom_call_target="tpu_custom_call" | custom-call | tf_op jit(solution)/shard_map/cond/branch_0_fun/track/pallas_call | solution.py:553
  (13 shorter events, 0.1 us)
Async XLA Ops:
  0.6 105.4 %copy-start.4 = (bf16[32,1024]{1,0:T(8,128)(2,1)S(1)}, bf16[32,1024]{1,0:T(8,128)(2,1)}, u32[]{:S(2)}) copy-start(bf16[32,1024]{1,0:T(8,128)(2,1)} %embed_ref.1) | copy-start | bytes 196612
  0.6 105.4 %copy-start.5 = (bf16[512,10]{0,1:T(8,128)(2,1)S(1)}, bf16[512,10]{0,1:T(8,128)(2,1)}, u32[]{:S(2)}) copy-start(bf16[512,10]{0,1:T(8,128)(2,1)} %param.27) | copy-start | bytes 30724
  0.7 105.4 %copy-start.8 = (f32[512]{0:T(512)S(1)}, f32[512]{0:T(512)}, u32[]{:S(2)}) copy-start(f32[512]{0:T(512)} %param.26) | copy-start | bytes 6148
  0.7 105.4 %copy-start.7 = (f32[1024]{0:T(1024)S(1)}, f32[1024]{0:T(1024)}, u32[]{:S(2)}) copy-start(f32[1024]{0:T(1024)} %param.24) | copy-start | bytes 12292
  0.7 105.4 %copy-start.9 = (f32[8]{0:T(128)S(1)}, f32[8]{0:T(128)}, u32[]{:S(2)}) copy-start(f32[8]{0:T(128)} %param.22) | copy-start | bytes 100
  0.7 105.4 %copy-start.6 = (f32[1024]{0:T(1024)S(1)}, f32[1024]{0:T(1024)}, u32[]{:S(2)}) copy-start(f32[1024]{0:T(1024)} %param.20) | copy-start | bytes 12292
  6.2 1.2 %copy-start.1 = (bf16[1,1,512,1024]{3,2,1,0:T(8,128)(2,1)S(1)}, bf16[1,1,512,1024]{3,2,1,0:T(8,128)(2,1)}, u32[]{:S(2)}) copy-start(bf16[1,1,512,1024]{3,2,1,0:T(8,128)(2,1)} %param.18) | copy-start | bytes 3145732
  7.4 98.7 %copy-start.2 = (bf16[1024,1024]{1,0:T(8,128)(2,1)S(1)}, bf16[1024,1024]{1,0:T(8,128)(2,1)}, u32[]{:S(2)}) copy-start(bf16[1024,1024]{1,0:T(8,128)(2,1)} %param.23) | copy-start | bytes 6291460
